TPU v7x, 256 devices: a whole 4x4x8 slice. The times are simulated.
256 devices in a mesh: gx: 32 (over z, y), gy: 4 (over x_hi, core), role: 2 (over x_lo).
Axes of the slice: x: 4 (x_hi: 2, x_lo: 2; x = x_hi * 2 + x_lo), y: 4, z: 8, core: 2. Of those that a mesh axis runs over, the one named last changes fastest.
Arguments:
- velocity: float32 [3, 512, 64, 256], P(None, 'gx', 'gy', 'role'), may hold values from -6 to 6
- target_visc: bfloat16 [256, 32, 128], P('gx', 'gy', 'role'), may hold values from 0.049804688 to 1
- w_first: bfloat16 [64, 81], replicated, may hold values from -2 to 2
- w_hidden: bfloat16 [64, 1728], replicated, may hold values from -0.3125 to 0.3125
- w_last: bfloat16 [64], replicated, may hold values from -1.5 to 1.5
- sample_owner: int32 [4, 2, 256, 1], P('gy', 'role'), may hold values from 0 to 31; in each aligned block of 8 rows (0 to 7, 8 to 15, ..., all dimensions but the last counted through in order) at most 2 rows name the same one
- sample_block: int32 [4, 2, 256, 1], P('gy', 'role'), may hold values from 0 to 7
Outputs:
- u_next: float32 [3, 512, 64, 256], P(None, 'gx', 'gy', 'role')
- slot_loss: float32 [4, 2, 256], P('gy', 'role', 'gx')
- grad_first: float32 [64, 81], replicated
- grad_hidden: float32 [64, 1728], replicated
- grad_last: float32 [64], replicated
Inputs may be any that keep to these rules, and one draw needn't show every extreme that they name: `sample_owner`: within one trainer's 8 rows (aligned blocks of rows) no gx index is named more than 2 times.
All inputs are finite; a program needn't handle non-finite values.
Results may differ from a plain program's by a relative error of at most 0.002.
The roundings to bfloat16 on the way count: a program that leaves them out, or rounds other values in their place, can miss the bound.
Values may be sent and summed in bfloat16 or wider, within the bound.
A program may use at most 128 MiB of HBM per device.

v0:
```python
import jax
import jax.numpy as jnp
from jax import lax
from jax.sharding import PartitionSpec as P

BSIDE = 8


base_visc = 0.02
time_step = 0.2


def padded_2(block, sides, width):
    for axis, dim in sides:
        count = lax.axis_size(axis)
        forward = [(i, i + 1) for i in range(count - 1)]
        forward.append((count - 1, 0))
        backward = [(target, source) for source, target in forward]
        low = lax.ppermute(
            lax.slice_in_dim(block, block.shape[dim] - width, None, axis=dim), axis, forward
        )
        high = lax.ppermute(lax.slice_in_dim(block, 0, width, axis=dim), axis, backward)
        block = jnp.concatenate([low, block, high], axis=dim)
    return block


def cell_masks(side):
    count = side**3
    flat = jnp.arange(count, dtype=jnp.int32)
    first = flat // (side * side)
    second = flat // side % side
    third = flat % side
    rows = []
    for k in range(27):
        shift_x = k // 9 - 1
        shift_y = k // 3 % 3 - 1
        shift_z = k % 3 - 1
        inside = (first + shift_x >= 0) & (first + shift_x < side)
        inside = inside & (second + shift_y >= 0) & (second + shift_y < side)
        inside = inside & (third + shift_z >= 0) & (third + shift_z < side)
        rows.append(inside)
    return jnp.stack(rows).astype(jnp.bfloat16)


def pad_cells(field, side):
    reach = side * side + side + 1
    return jnp.pad(field, ((0, 0), (0, 0), (reach, reach)))


def shifted(padded, masks, side, k, count):
    reach = side * side + side + 1
    offset = (k // 9 - 1) * side * side + (k // 3 % 3 - 1) * side + (k % 3 - 1)
    return lax.slice_in_dim(padded, reach + offset, reach + offset + count, axis=2) * masks[k]


def convolve(weight, field, masks, side):
    inner = field.shape[1]
    count = field.shape[2]
    padded = pad_cells(field, side)
    summed = None
    for k in range(27):
        term = jnp.einsum(
            "oc,bcn->bon",
            weight[:, k * inner : (k + 1) * inner],
            shifted(padded, masks, side, k, count),
            preferred_element_type=jnp.float32,
        )
        summed = term if summed is None else summed + term
    return summed


def silu_slope(value):
    sig = jax.nn.sigmoid(value)
    return sig * (1.0 + value * (1.0 - sig))


def network(w_first, w_hidden, w_last, inputs, masks, side):
    pre_first = convolve(w_first, inputs, masks, side)
    act_first = jax.nn.silu(pre_first).astype(jnp.bfloat16)
    pre_hidden = convolve(w_hidden, act_first, masks, side)
    act_hidden = jax.nn.silu(pre_hidden).astype(jnp.bfloat16)
    logits = jnp.einsum("c,bcn->bn", w_last, act_hidden, preferred_element_type=jnp.float32)
    eddy = 0.5 * jax.nn.softplus(logits)
    return (pre_first, act_first, pre_hidden, act_hidden, logits, eddy)


def fit_blocks(w_first, w_hidden, w_last, blocks, masks, side, trainers):
    count = blocks.shape[2]
    width = w_hidden.shape[0]
    inputs = blocks[:, :3]
    target = blocks[:, 3].astype(jnp.float32)
    pre_first, act_first, pre_hidden, act_hidden, logits, eddy = network(
        w_first, w_hidden, w_last, inputs, masks, side
    )
    error = eddy - target
    losses = jnp.mean(error * error, axis=1)
    d_logit = (error * jax.nn.sigmoid(logits) / (trainers * count)).astype(jnp.bfloat16)
    grad_last = jnp.einsum("bn,bcn->c", d_logit, act_hidden, preferred_element_type=jnp.float32)
    d_hidden = (
        w_last.astype(jnp.float32)[None, :, None]
        * d_logit.astype(jnp.float32)[:, None, :]
        * silu_slope(pre_hidden)
    ).astype(jnp.bfloat16)
    padded_act = pad_cells(act_first, side)
    grad_hidden = jnp.concatenate(
        [
            jnp.einsum(
                "bon,bcn->oc",
                d_hidden,
                shifted(padded_act, masks, side, k, count),
                preferred_element_type=jnp.float32,
            )
            for k in range(27)
        ],
        axis=1,
    )
    padded_delta = pad_cells(d_hidden, side)
    d_act = None
    for k in range(27):
        term = jnp.einsum(
            "oc,bon->bcn",
            w_hidden[:, k * width : (k + 1) * width],
            shifted(padded_delta, masks, side, 26 - k, count),
            preferred_element_type=jnp.float32,
        )
        d_act = term if d_act is None else d_act + term
    d_first = (d_act * silu_slope(pre_first)).astype(jnp.bfloat16)
    padded_in = pad_cells(inputs, side)
    grad_first = jnp.concatenate(
        [
            jnp.einsum(
                "bon,bcn->oc",
                d_first,
                shifted(padded_in, masks, side, k, count),
                preferred_element_type=jnp.float32,
            )
            for k in range(27)
        ],
        axis=1,
    )
    return (losses, grad_first, grad_hidden, grad_last)


def to_blocks(field, side):
    chans, size_x, size_y, size_z = field.shape
    split = field.reshape(chans, size_x // side, side, size_y // side, side, size_z // side, side)
    return split.transpose(1, 3, 5, 0, 2, 4, 6).reshape(-1, chans, side**3)


def from_blocks(values, size_x, size_y, size_z, side):
    split = values.reshape(size_x // side, size_y // side, size_z // side, side, side, side)
    return split.transpose(0, 3, 1, 4, 2, 5).reshape(size_x, size_y, size_z)


def window(padded, axis, shift, reach, lead):
    bounds = []
    for dim in range(padded.ndim):
        if dim < lead:
            bounds.append(slice(None))
        else:
            length = padded.shape[dim] - 2 * reach
            opening = reach + (shift if dim == axis else 0)
            bounds.append(slice(opening, opening + length))
    return padded[tuple(bounds)]


def on_device(velocity, target_visc, w_first, w_hidden, w_last, sample_owner, sample_block):
    side = BSIDE
    masks = cell_masks(side)
    comps, cells_x, cells_y, cells_z = velocity.shape
    half_x, half_y, half_z = (cells_x // 2, cells_y // 2, cells_z // 2)
    filtered = (
        velocity.reshape(3, half_x, 2, half_y, 2, half_z, 2)
        .mean(axis=(2, 4, 6))
        .astype(jnp.bfloat16)
    )
    vel_blocks = to_blocks(filtered, side)
    target_blocks = to_blocks(target_visc[None], side)
    stacked = jnp.concatenate([vel_blocks, target_blocks], axis=1)
    eddy = network(w_first, w_hidden, w_last, vel_blocks, masks, side)[5]
    eddy_field = from_blocks(eddy, half_x, half_y, half_z, side)
    eddy_rim = padded_2(eddy_field, (("gx", 0), ("gy", 1), ("role", 2)), 1)
    fine_rim = jnp.repeat(jnp.repeat(jnp.repeat(eddy_rim, 2, 0), 2, 1), 2, 2)
    visc_pad = base_visc + fine_rim[1:-1, 1:-1, 1:-1]
    visc = window(visc_pad, 0, 0, 1, 0)
    vel_pad = padded_2(velocity, (("gx", 1), ("gy", 2), ("role", 3)), 2)
    advect = jnp.zeros_like(velocity)
    diffuse = jnp.zeros_like(velocity)
    for axis in range(3):
        dim = axis + 1
        ahead_one = window(vel_pad, dim, 1, 2, 1)
        behind_one = window(vel_pad, dim, -1, 2, 1)
        ahead_two = window(vel_pad, dim, 2, 2, 1)
        behind_two = window(vel_pad, dim, -2, 2, 1)
        slope = (8.0 * (ahead_one - behind_one) - (ahead_two - behind_two)) / 12.0
        advect = advect + velocity[axis][None] * slope
        visc_ahead = 0.5 * (visc + window(visc_pad, axis, 1, 1, 0))
        visc_behind = 0.5 * (visc + window(visc_pad, axis, -1, 1, 0))
        diffuse = (
            diffuse
            + visc_ahead[None] * (ahead_one - velocity)
            - visc_behind[None] * (velocity - behind_one)
        )
    u_next = velocity + time_step * (diffuse - advect)
    groups = lax.axis_size("gx")
    trainers = groups * lax.axis_size("gy") * lax.axis_size("role")
    slots = sample_owner.shape[2] // groups
    held = stacked.shape[0]
    my_index = lax.axis_index("gx")
    owners = sample_owner.reshape(groups, slots)
    picks = sample_block.reshape(groups, slots)
    my_owners = lax.dynamic_index_in_dim(owners, my_index, 0, keepdims=False)
    my_picks = lax.dynamic_index_in_dim(picks, my_index, 0, keepdims=False)
    wanted = my_owners * held + my_picks
    piece = lax.all_gather(stacked, "gx", axis=0, tiled=True)
    rows = piece.shape[0]
    onehot = (wanted[:, None] == jnp.arange(rows, dtype=jnp.int32)[None, :]).astype(jnp.bfloat16)
    received = jnp.einsum("sr,rcn->scn", onehot, piece, preferred_element_type=jnp.float32).astype(
        jnp.bfloat16
    )
    losses, grad_first, grad_hidden, grad_last = fit_blocks(
        w_first, w_hidden, w_last, received, masks, side, trainers
    )
    grad_first, grad_hidden, grad_last = lax.psum(
        (grad_first, grad_hidden, grad_last), ("gx", "gy", "role")
    )
    slot_loss = losses.reshape(1, 1, slots)
    return (u_next, slot_loss, grad_first, grad_hidden, grad_last)


def solution(mesh):
    return jax.shard_map(
        on_device,
        mesh=mesh,
        in_specs=(
            P(None, "gx", "gy", "role"),
            P("gx", "gy", "role"),
            P(),
            P(),
            P(),
            P("gy", "role", None, None),
            P("gy", "role", None, None),
        ),
        out_specs=(P(None, "gx", "gy", "role"), P("gy", "role", "gx"), P(), P(), P()),
        check_vma=False,
    )
```

profile of v0, /device:TPU:1, one launch (start us, length us, event | category | flops | bytes accessed | tf_op | source)
XLA Modules:
  0.0 471.1 jit_solution(11536590155366715147)
XLA Ops:
  7.2 27.3 %reshape.554 = f32[3,8,2,8,2,64,2]{6,5,4,3,2,1,0:T(8,128)} reshape(f32[3,16,16,128]{3,2,1,0:T(8,128)} %param.7) | data formatting | bytes 786432 | tf_op jit(solution)/shard_map/reshape | solution.py:173
  34.5 9.4 %reduce_sum.18 = f32[3,8,8,64]{3,2,1,0:T(8,128)S(1)} reduce(f32[3,8,2,8,2,64,2]{6,5,4,3,2,1,0:T(8,128)} %reshape.554, f32[]{:T(128)} %constant.188.clone.1), dimensions={2,4,6}, to_apply=%region_0.1 | reduce | flops 86016 | bytes 442372 | tf_op jit(solution)/shard_map/reduce_sum | solution.py:174
  58.9 1.4 convolution_bitcast_fusion.12
  60.3 1.4 convolution_bitcast_fusion.13
  61.7 1.4 convolution_bitcast_fusion.14
  64.4 1.4 convolution_bitcast_fusion.16
  65.8 1.4 convolution_bitcast_fusion.17
  67.1 1.4 convolution_bitcast_fusion.18
  76.4 4.4 fusion.57
  81.3 2.1 collective-permute-start
  83.5 6.8 %collective-permute-start.1 = (f32[1,8,64]{2,1,0:T(8,128)S(1)}, f32[1,8,64]{2,1,0:T(8,128)S(1)}, u32[]{:S(2)}, u32[]{:S(2)}) collective-permute-start(f32[1,8,64]{2,1,0:T(8,128)S(1)} %slice.1200), channel_id=1, source_target_pairs={{8,0},{16,8},{24,16},{32,24},{40,32},{48,40},{56,48},{64,56},{72,6... | collective-permute-start | bytes 6152 | tf_op jit(solution)/shard_map/ppermute | solution.py:22
  90.4 4.8 %collective-permute-start.6 = (f32[3,2,16,128]{3,2,1,0:T(8,128)S(1)}, f32[3,2,16,128]{3,2,1,0:T(8,128)}, u32[]{:S(2)}, u32[]{:S(2)}) collective-permute-start(f32[3,2,16,128]{3,2,1,0:T(8,128)S(1)} %get-tuple-element.87), channel_id=1, source_target_pairs={{8,0},{16,8},{24,16},{32,24},{40,32},{48,40},{56,48},{64,56},{72,6... | collective-permute-start | bytes 147464 | tf_op jit(solution)/shard_map/ppermute | solution.py:22
  95.3 4.2 collective-permute-start.2
  102.4 1.8 collective-permute-done.3
  104.6 1.4 collective-permute-start.5
  108.2 1.6 collective-permute-done.5
  111.0 2.0 reshape.560
  113.0 1.7 slice.1347
  117.2 2.3 collective-permute-start.9
  119.7 3.4 copy.983
  123.1 3.3 copy.982
  126.4 3.3 copy.984
  129.8 7.6 %pad_maximum_fusion = f32[3,20,20,128]{2,1,3,0:T(8,128)S(1)} fusion(f32[3,20,2,128]{2,1,3,0:T(8,128)} %copy.984, f32[3,20,16,128]{2,1,3,0:T(8,128)} %copy.983, f32[3,20,2,128]{2,1,3,0:T(8,128)} %copy.982), kind=kLoop, calls=%fused_computation | loop fusion | flops 307200 | bytes 1228800 | tf_op jit(solution)/shard_map/concatenate | solution.py:23
  137.4 2.1 copy-done.1
  142.8 4.1 copy.985
  149.6 2.2 copy.987
  151.9 3.9 fusion.204
  155.7 1.5 convolution_convert_fusion
  204.8 1.8 fusion.56
  215.3 74.4 %all-reduce.5 = (f32[64,81]{0,1:T(8,128)S(1)}, f32[64]{0:T(128)}) all-reduce(f32[64,81]{0,1:T(8,128)S(1)} %concatenate.61, f32[64]{0:T(128)S(1)} %convolution_bitcast_fusion.104), channel_id=1, replica_groups=mesh['gx'=32,'gy'=4,'role'=2] {'gx','gy','role'}, use_global_device_ids=true, to_apply=%region_2.3 | all-reduce | flops 5248 | bytes 41984 | tf_op jit(solution)/shard_map/psum | solution.py:224
  290.9 171.2 %all-reduce.8.cloned.1.call-done = f32[64,1728]{1,0:T(8,128)} async-done(((f32[64,1728]{1,0:T(8,128)}), f32[64,1728]{1,0:T(8,128)}) %all-reduce.8.cloned.1.call-update) | async-done | bytes 442384 | tf_op jit(solution)/shard_map/psum | solution.py:224
  462.2 1.8 copy.1344
  (389 shorter events, 95.6 us)
Async XLA Ops:
  7.2 148.5 %all-gather.2.cloned.1.call-start = ((), (), s32[]{:S(2)}) async-start(), calls=%async_computation | async-start | bytes 1081344 | tf_op jit(solution)/shard_map/all_gather | solution.py:215
  45.8 416.3 %all-reduce.8.cloned.1.call-start = ((), (), s32[]{:S(2)}) async-start(), calls=%async_computation.1 | async-start | bytes 917504 | tf_op jit(solution)/shard_map/psum | solution.py:224
  47.1 14.5 %copy-start.35 = (bf16[512]{0:T(512)(128)(2,1)}, bf16[512]{0:T(512)(128)(2,1)S(1)}, u32[]{:S(2)}) copy-start(bf16[512]{0:T(512)(128)(2,1)S(1)} %get-tuple-element.44) | copy-start | bytes 3076
  47.1 15.9 %copy-start.33 = (bf16[512]{0:T(512)(128)(2,1)}, bf16[512]{0:T(512)(128)(2,1)S(1)}, u32[]{:S(2)}) copy-start(bf16[512]{0:T(512)(128)(2,1)S(1)} %get-tuple-element.45) | copy-start | bytes 3076
  47.2 17.2 %copy-start.31 = (bf16[512]{0:T(512)(128)(2,1)}, bf16[512]{0:T(512)(128)(2,1)S(1)}, u32[]{:S(2)}) copy-start(bf16[512]{0:T(512)(128)(2,1)S(1)} %get-tuple-element.46) | copy-start | bytes 3076
  47.2 18.6 %copy-start.29 = (bf16[512]{0:T(512)(128)(2,1)}, bf16[512]{0:T(512)(128)(2,1)S(1)}, u32[]{:S(2)}) copy-start(bf16[512]{0:T(512)(128)(2,1)S(1)} %get-tuple-element.47) | copy-start | bytes 3076
  47.2 20.0 %copy-start.27 = (bf16[512]{0:T(512)(128)(2,1)}, bf16[512]{0:T(512)(128)(2,1)S(1)}, u32[]{:S(2)}) copy-start(bf16[512]{0:T(512)(128)(2,1)S(1)} %get-tuple-element.48) | copy-start | bytes 3076
  47.2 21.3 %copy-start.43 = (bf16[512]{0:T(512)(128)(2,1)}, bf16[512]{0:T(512)(128)(2,1)S(1)}, u32[]{:S(2)}) copy-start(bf16[512]{0:T(512)(128)(2,1)S(1)} %get-tuple-element.40) | copy-start | bytes 3076
  47.2 25.6 %copy-start.11 = (bf16[512]{0:T(512)(128)(2,1)}, bf16[512]{0:T(512)(128)(2,1)S(1)}, u32[]{:S(2)}) copy-start(bf16[512]{0:T(512)(128)(2,1)S(1)} %get-tuple-element.58) | copy-start | bytes 3076
  47.2 29.1 %copy-start.9 = (bf16[512]{0:T(512)(128)(2,1)}, bf16[512]{0:T(512)(128)(2,1)S(1)}, u32[]{:S(2)}) copy-start(bf16[512]{0:T(512)(128)(2,1)S(1)} %get-tuple-element.49) | copy-start | bytes 3076
  47.3 22.6 %copy-start.25 = (bf16[512]{0:T(512)(128)(2,1)}, bf16[512]{0:T(512)(128)(2,1)S(1)}, u32[]{:S(2)}) copy-start(bf16[512]{0:T(512)(128)(2,1)S(1)} %get-tuple-element.65) | copy-start | bytes 3076
  47.3 23.0 %copy-start.23 = (bf16[512]{0:T(512)(128)(2,1)}, bf16[512]{0:T(512)(128)(2,1)S(1)}, u32[]{:S(2)}) copy-start(bf16[512]{0:T(512)(128)(2,1)S(1)} %get-tuple-element.64) | copy-start | bytes 3076
  47.3 23.4 %copy-start.21 = (bf16[512]{0:T(512)(128)(2,1)}, bf16[512]{0:T(512)(128)(2,1)S(1)}, u32[]{:S(2)}) copy-start(bf16[512]{0:T(512)(128)(2,1)S(1)} %get-tuple-element.63) | copy-start | bytes 3076
  47.3 23.8 %copy-start.19 = (bf16[512]{0:T(512)(128)(2,1)}, bf16[512]{0:T(512)(128)(2,1)S(1)}, u32[]{:S(2)}) copy-start(bf16[512]{0:T(512)(128)(2,1)S(1)} %get-tuple-element.62) | copy-start | bytes 3076
  47.3 24.3 %copy-start.17 = (bf16[512]{0:T(512)(128)(2,1)}, bf16[512]{0:T(512)(128)(2,1)S(1)}, u32[]{:S(2)}) copy-start(bf16[512]{0:T(512)(128)(2,1)S(1)} %get-tuple-element.61) | copy-start | bytes 3076
  47.3 24.7 %copy-start.15 = (bf16[512]{0:T(512)(128)(2,1)}, bf16[512]{0:T(512)(128)(2,1)S(1)}, u32[]{:S(2)}) copy-start(bf16[512]{0:T(512)(128)(2,1)S(1)} %get-tuple-element.60) | copy-start | bytes 3076
  47.3 25.1 %copy-start.13 = (bf16[512]{0:T(512)(128)(2,1)}, bf16[512]{0:T(512)(128)(2,1)S(1)}, u32[]{:S(2)}) copy-start(bf16[512]{0:T(512)(128)(2,1)S(1)} %get-tuple-element.59) | copy-start | bytes 3076
  76.4 13.9 %copy-start.3 = (f32[3,16,16,128]{3,2,1,0:T(8,128)S(1)}, f32[3,16,16,128]{3,2,1,0:T(8,128)}, u32[]{:S(2)}) copy-start(f32[3,16,16,128]{3,2,1,0:T(8,128)} %param.7) | copy-start | bytes 1179652
  76.4 24.5 %copy-start.50 = (s32[1,1,256,1]{2,3,1,0:T(1,128)S(1)}, s32[1,1,256,1]{2,3,1,0:T(1,128)}, u32[]{:S(2)}) copy-start(s32[1,1,256,1]{2,3,1,0:T(1,128)} %param.12) | copy-start | bytes 3076
  76.4 25.2 %copy-start.51 = (s32[1,1,256,1]{2,3,1,0:T(1,128)S(1)}, s32[1,1,256,1]{2,3,1,0:T(1,128)}, u32[]{:S(2)}) copy-start(s32[1,1,256,1]{2,3,1,0:T(1,128)} %param.13) | copy-start | bytes 3076
  81.3 14.0 %collective-permute-start = (f32[1,8,64]{2,1,0:T(8,128)S(1)}, f32[1,8,64]{2,1,0:T(8,128)S(1)}, u32[]{:S(2)}, u32[]{:S(2)}) collective-permute-start(f32[1,8,64]{2,1,0:T(8,128)S(1)} %slice.1198), channel_id=1, source_target_pairs={{0,8},{8,16},{16,24},{24,32},{32,40},{40,48},{48,56},{56,64},{64,7... | collective-permute-start | bytes 6152 | tf_op jit(solution)/shard_map/ppermute | solution.py:19
  83.5 11.8 %collective-permute-start.1 = (f32[1,8,64]{2,1,0:T(8,128)S(1)}, f32[1,8,64]{2,1,0:T(8,128)S(1)}, u32[]{:S(2)}, u32[]{:S(2)}) collective-permute-start(f32[1,8,64]{2,1,0:T(8,128)S(1)} %slice.1200), channel_id=1, source_target_pairs={{8,0},{16,8},{24,16},{32,24},{40,32},{48,40},{56,48},{64,56},{72,6... | collective-permute-start | bytes 6152 | tf_op jit(solution)/shard_map/ppermute | solution.py:22
  90.3 25.1 %collective-permute-start.7 = (f32[3,2,16,128]{3,2,1,0:T(8,128)S(1)}, f32[3,2,16,128]{3,2,1,0:T(8,128)}, u32[]{:S(2)}, u32[]{:S(2)}) collective-permute-start(f32[3,2,16,128]{3,2,1,0:T(8,128)S(1)} %get-tuple-element.88), channel_id=1, source_target_pairs={{0,8},{8,16},{16,24},{24,32},{32,40},{40,48},{48,56},{56,64},{64,7... | collective-permute-start | bytes 147464 | tf_op jit(solution)/shard_map/ppermute | solution.py:19
  90.4 26.0 %collective-permute-start.6 = (f32[3,2,16,128]{3,2,1,0:T(8,128)S(1)}, f32[3,2,16,128]{3,2,1,0:T(8,128)}, u32[]{:S(2)}, u32[]{:S(2)}) collective-permute-start(f32[3,2,16,128]{3,2,1,0:T(8,128)S(1)} %get-tuple-element.87), channel_id=1, source_target_pairs={{8,0},{16,8},{24,16},{32,24},{40,32},{48,40},{56,48},{64,56},{72,6... | collective-permute-start | bytes 147464 | tf_op jit(solution)/shard_map/ppermute | solution.py:22
  95.3 7.0 %collective-permute-start.2 = (f32[10,1,64]{2,1,0:T(1,128)S(1)}, f32[10,1,64]{2,1,0:T(1,128)S(1)}, u32[]{:S(2)}, u32[]{:S(2)}) collective-permute-start(f32[10,1,64]{2,1,0:T(1,128)S(1)} %get-tuple-element.98), channel_id=1, source_target_pairs={{0,2},{2,4},{4,6},{6,0},{1,3},{3,5},{5,7},{7,1},{8,10},{10,12},{12... | collective-permute-start | bytes 7688 | tf_op jit(solution)/shard_map/ppermute | solution.py:19
  99.6 4.5 collective-permute-start.3
  104.2 3.9 collective-permute-start.4
  104.6 5.2 %collective-permute-start.5 = (f32[10,10,1]{2,1,0:T(8,128)S(1)}, f32[10,10,1]{2,1,0:T(8,128)S(1)}, u32[]{:S(2)}, u32[]{:S(2)}) collective-permute-start(f32[10,10,1]{2,1,0:T(8,128)S(1)} %get-tuple-element.92), channel_id=1, source_target_pairs={{1,0},{0,1},{3,2},{2,3},{5,4},{4,5},{7,6},{6,7},{9,8},{8,9},{11,10... | collective-permute-start | bytes 1208 | tf_op jit(solution)/shard_map/ppermute | solution.py:22
  117.2 5.9 %collective-permute-start.9 = (f32[3,20,2,128]{3,1,2,0:T(8,128)S(1)}, f32[3,20,2,128]{3,1,2,0:T(8,128)S(1)}, u32[]{:S(2)}, u32[]{:S(2)}) collective-permute-start(f32[3,20,2,128]{3,1,2,0:T(8,128)S(1)} %copy.1158), channel_id=1, source_target_pairs={{0,2},{2,4},{4,6},{6,0},{1,3},{3,5},{5,7},{7,1},{8,10},{10,12},{12... | collective-permute-start | bytes 184328 | tf_op jit(solution)/shard_map/ppermute | solution.py:19
  119.5 6.9 %collective-permute-start.8 = (f32[3,20,2,128]{3,1,2,0:T(8,128)S(1)}, f32[3,20,2,128]{3,1,2,0:T(8,128)S(1)}, u32[]{:S(2)}, u32[]{:S(2)}) collective-permute-start(f32[3,20,2,128]{3,1,2,0:T(8,128)S(1)} %copy.1157), channel_id=1, source_target_pairs={{2,0},{4,2},{6,4},{0,6},{3,1},{5,3},{7,5},{1,7},{10,8},{12,10},{14... | collective-permute-start | bytes 184328 | tf_op jit(solution)/shard_map/ppermute | solution.py:22
  140.2 8.1 %collective-permute-start.10 = (f32[3,20,20,2]{2,1,3,0:T(8,128)S(1)}, f32[3,20,20,2]{2,1,3,0:T(8,128)}, u32[]{:S(2)}, u32[]{:S(2)}) collective-permute-start(f32[3,20,20,2]{2,1,3,0:T(8,128)S(1)} %get-tuple-element.71), channel_id=1, source_target_pairs={{1,0},{0,1},{3,2},{2,3},{5,4},{4,5},{7,6},{6,7},{9,8},{8,9},{11,10... | collective-permute-start | bytes 28808 | tf_op jit(solution)/shard_map/ppermute | solution.py:22
  140.4 9.2 %collective-permute-start.11 = (f32[3,20,20,2]{2,1,3,0:T(8,128)}, f32[3,20,20,2]{2,1,3,0:T(8,128)}, u32[]{:S(2)}, u32[]{:S(2)}) collective-permute-start(f32[3,20,20,2]{2,1,3,0:T(8,128)} %get-tuple-element.72), channel_id=1, source_target_pairs={{0,1},{1,0},{2,3},{3,2},{4,5},{5,4},{6,7},{7,6},{8,9},{9,8},{10,11... | collective-permute-start | bytes 28808 | tf_op jit(solution)/shard_map/ppermute | solution.py:19
  (35 other events, 160.1 us)
Sparse Core Ops, SparseCore 0:
  45.9 70.8 all-gather.1
  214.4 247.7 all-reduce.7
where the time goes:
time: 475 us; the launch traced here: 471 us
  waiting for transfers between devices  176 us (37%)
  matrix products  86.1 us (18%)
  blocking collectives  74.4 us (16%)
  local copies, waits for them, and re-layouts  63.8 us (13%)
  other arithmetic  30.2 us (6%)
  starting transfers between devices  24.2 us (5%)
  between operations  16.6 us (3%)
    psum x1, waiting for transfers between devices, on_device(): lax.psum((grad_first, grad_hidden, grad_last), ('gx', 'gy', 'role'))  171 us
    psum x1, blocking collectives, on_device(): lax.psum((grad_first, grad_hidden, grad_last), ('gx', 'gy', 'role'))  74.4 us
    dot_general x107, matrix products, convolve(): jnp.einsum('oc,bcn->bon', weight[:, k * inner:(k + 1) * inner], shifted(p...  49.1 us
    reshape x1, local copies, waits for them, and re-layouts, on_device(): velocity.reshape(3, half_x, 2, half_y, 2, half_z, 2).mean(axis=(2, 4, 6))  27.3 us
    dot_general x27, matrix products, fit_blocks(): jnp.einsum('oc,bon->bcn', w_hidden[:, k * width:(k + 1) * width], shifted...  13.7 us
    ppermute x6, starting transfers between devices, padded_2(): lax.ppermute(lax.slice_in_dim(block, 0, width, axis=dim), axis, backward)  13.2 us
    ppermute x6, starting transfers between devices, padded_2(): lax.ppermute(lax.slice_in_dim(block, block.shape[dim] - width, None, axis...  10.4 us
    dot_general x27, matrix products, fit_blocks(): jnp.einsum('bon,bcn->oc', d_hidden, shifted(padded_act, masks, side, k, c...  10.1 us
  transfers between devices with their start and end apart: 14, of which 4 were waited for; matrix products, arithmetic and copies ran while one was open for 17% of the time, Pallas kernels for 0%

commit v1 on v0

v1 whole, which is shorter than its diff:
```python
import numpy as np
import jax
import jax.numpy as jnp
from jax import lax
from jax.sharding import PartitionSpec as P
from jax.experimental import pallas as pl
from jax.experimental.pallas import tpu as pltpu

SIDE = 8
CH = 64
F32 = jnp.float32
BF16 = jnp.bfloat16
NT = (((1,), (1,)), ((), ()))
NN = (((1,), (0,)), ((), ()))


def dot(a, b, dims=NN):
    return lax.dot_general(a, b, dims, preferred_element_type=F32)


def pool_matrix():
    z = np.arange(128)[:, None]
    lane = np.arange(256)[None, :]
    block, inner = lane // 32, lane % 32
    parts = []
    for comp in range(3):
        hit = (inner < 24) & (inner % 3 == comp) & (z // 2 == block * 8 + inner // 3)
        parts.append(np.where(hit, 0.125, 0.0))
    return np.concatenate(parts, 0).astype(jnp.bfloat16)


def target_matrix():
    z = np.arange(64)[:, None]
    lane = np.arange(256)[None, :]
    block, inner = lane // 32, lane % 32
    return ((inner >= 24) & (z == block * 8 + inner - 24)).astype(jnp.bfloat16)


def spread_matrix():
    row = np.arange(128)[:, None]
    lane = np.arange(512)[None, :]
    return (row == 24 + lane // 64).astype(jnp.bfloat16)


def first_selector():
    out = np.zeros((81, 3, 8, 128), np.float32)
    for i in range(3):
        for zo in range(8):
            for j in range(3):
                for t in range(9):
                    zi = zo - 1 + t // 3
                    if 0 <= zi < 8:
                        out[9 * (3 * i + j) + t, i, zo, j * 32 + zi * 3 + t % 3] = 1.0
    return out.reshape(81, 3072).astype(jnp.bfloat16)


def lane_of(shape):
    return lax.broadcasted_iota(jnp.int32, shape, len(shape) - 1)


def shift_y(field, shift):
    zero = jnp.zeros((8, 8, field.shape[2]), field.dtype)
    if shift < 0:
        return jnp.concatenate([zero, field[:, :56]], axis=1)
    if shift > 0:
        return jnp.concatenate([field[:, 8:], zero], axis=1)
    return field


def widen(store, field):
    lane = lane_of((512, 128))
    zero = jnp.zeros((64, 1152), BF16)
    near = [
        jnp.where(lane >= 64, pltpu.roll(field[:, 256:384], 64, 1), 0.0),
        jnp.where(lane < 64, pltpu.roll(field[:, 128:256], 64, 1), 0.0),
    ]
    for half in range(2):
        store[half, 0] = zero
        store[half, 9] = zero
        whole = jnp.concatenate([field[:, half * 256 : half * 256 + 256], near[half]], axis=1)
        whole = whole.reshape(8, 64, 384)
        for j in range(3):
            store[half, 1:9, :, j * 384 : (j + 1) * 384] = shift_y(whole, j - 1).astype(BF16)


def rows_of(store, half, i):
    return store[half, i : i + 8].reshape(512, 1152)


def place_weights(w_hidden, ahead, back):
    lane = lane_of((64, 128))
    low = lane < 64
    zero = jnp.zeros((64, 128), BF16)
    tiles = [w_hidden[:, t * 128 : (t + 1) * 128] for t in range(13)]
    last = w_hidden[:, 1664:1728]
    tiles.append(jnp.concatenate([last, last], axis=1))
    tiles = [t.astype(F32) for t in tiles]
    swapped = [pltpu.roll(t, 64, 1) for t in tiles]
    for j in range(9):
        t = 3 * j // 2
        if j % 2 == 0:
            ab = tiles[t]
            bc = jnp.where(low, swapped[t], swapped[t + 1])
            c_low, c_high = tiles[t + 1], swapped[t + 1]
            a_low, a_high = tiles[t], swapped[t]
        else:
            bc = tiles[t + 1]
            ab = jnp.where(low, swapped[t], swapped[t + 1])
            c_low, c_high = swapped[t + 1], tiles[t + 1]
            a_low, a_high = swapped[t], tiles[t]
        c_0 = jnp.where(low, c_low, 0.0).astype(BF16)
        o_c = jnp.where(low, 0.0, c_high).astype(BF16)
        a_0 = jnp.where(low, a_low, 0.0).astype(BF16)
        o_a = jnp.where(low, 0.0, a_high).astype(BF16)
        ab = ab.astype(BF16)
        bc = bc.astype(BF16)
        rows = [(bc, zero, a_0), (ab, c_0, zero), (o_a, bc, zero), (zero, ab, o_c)]
        for zo in range(4):
            for part in range(3):
                start = (j % 3) * 384 + part * 128
                ahead[j // 3, zo * 64 : (zo + 1) * 64, start : start + 128] = rows[zo][part]
        flip = 8 - j
        rows = [(bc, zero), (ab, c_0), (o_a, bc), (zero, ab), (c_0, zero), (zero, o_a)]
        for zi in range(6):
            start = (flip % 3) * 384 + zi * 64
            for part in range(2):
                back[flip // 3, start : start + 64, part * 128 : (part + 1) * 128] = rows[zi][part]


def local_kernel(
    vel, target, w_first, w_hidden, w_last, owner, block, pool, tmat, spread, sel,
    sums, visc,
    filt, first_in, w_one, ahead, back, wide_act, wide_del, slope_one, slope_two, eddy_z,
):
    place_weights(w_hidden, ahead, back)
    placed = dot(w_first[...], sel[...]).astype(BF16)
    for i in range(3):
        for zo in range(8):
            at = (i * 8 + zo) * 128
            w_one[i, zo * 64 : (zo + 1) * 64, :] = placed[:, at : at + 128]

    pooled = []
    for comp in range(3):
        total = None
        for dx in range(2):
            for dy in range(2):
                part = jnp.concatenate(
                    [vel[comp, 2 * x + dx, pl.ds(dy, 8, stride=2), :] for x in range(8)], axis=0
                )
                total = part if total is None else total + part
        pooled.append(total)
    rest = jnp.concatenate(pooled, axis=1)
    blocks = None
    for _ in range(3):
        piece = rest.astype(BF16)
        rest = rest - piece.astype(F32)
        term = dot(piece, pool[...])
        blocks = term if blocks is None else blocks + term
    blocks = blocks.astype(BF16).astype(F32)
    want = target[...].astype(F32).reshape(64, 64).astype(BF16)
    blocks = blocks + dot(want, tmat[...])
    for b in range(8):
        tile = blocks[:, (b // 4) * 128 : (b // 4) * 128 + 128]
        if b % 4:
            tile = pltpu.roll(tile, 128 - 32 * (b % 4), 1)
        filt[pl.ds(b, 64, stride=8), :] = tile
    held = filt[...]
    targets = dot(held.astype(BF16), spread[...])
    lane = lane_of((512, 128))
    inputs = jnp.where(lane < 24, held, 0.0).reshape(8, 64, 128)
    near = shift_y(inputs, -1)
    near = near + pltpu.roll(inputs.reshape(512, 128), 32, 1).reshape(8, 64, 128)
    near = near + pltpu.roll(shift_y(inputs, 1).reshape(512, 128), 64, 1).reshape(8, 64, 128)
    first_in[0] = jnp.zeros((64, 128), BF16)
    first_in[9] = jnp.zeros((64, 128), BF16)
    first_in[1:9] = near.astype(BF16)

    pre = None
    for i in range(3):
        term = dot(first_in[i : i + 8].reshape(512, 128), w_one[i], NT)
        pre = term if pre is None else pre + term
    sig = 1.0 / (1.0 + jnp.exp(-pre))
    slope_one[...] = sig * (1.0 + pre * (1.0 - sig))
    widen(wide_act, (pre * sig).astype(BF16).astype(F32))

    wl = w_last[...].astype(F32)
    wl = jnp.concatenate([wl, wl, wl, wl], axis=1)
    rows_iota = lax.broadcasted_iota(jnp.int32, (384, 256), 0)
    lanes_iota = lax.broadcasted_iota(jnp.int32, (384, 256), 1)
    cell = jnp.where(rows_iota < 256, rows_iota // 64, (rows_iota // 2) % 4)
    out_map = jnp.where(cell == lanes_iota // 64, wl, 0.0).astype(BF16)

    mine = owner[...] == lax.axis_index("gx")
    number = lax.broadcasted_iota(jnp.int32, (8, 256), 0)
    drawn = jnp.where(mine & (block[...] == number), 1.0, 0.0)
    times = jnp.sum(drawn, axis=1, keepdims=True)

    loss = jnp.zeros((8, 256), F32)
    last = jnp.zeros((8, 256), F32)
    deltas, parts = [], []
    for half in range(2):
        pre = None
        for i in range(3):
            term = dot(rows_of(wide_act, half, i), ahead[i], NT)
            pre = term if pre is None else pre + term
        sig = 1.0 / (1.0 + jnp.exp(-pre))
        act = (pre * sig).astype(BF16)
        slope = sig * (1.0 + pre * (1.0 - sig))
        both = dot(act, out_map, NT)
        logits = both[:, :256]
        eddy_z[half] = 0.5 * (
            jnp.maximum(both[:, 256:], 0.0) + jnp.log1p(jnp.exp(-jnp.abs(both[:, 256:])))
        )
        small = jnp.exp(-jnp.abs(logits))
        eddy = 0.5 * (jnp.maximum(logits, 0.0) + jnp.log1p(small))
        gate = jnp.where(logits >= 0, 1.0, small) / (1.0 + small)
        error = eddy - targets[:, half * 256 : half * 256 + 256]
        loss = loss + jnp.sum((error * error).reshape(64, 8, 256), axis=0)
        d_logit = (error * gate * (1.0 / (256 * 512))).astype(BF16).astype(F32)
        last = last + jnp.sum((d_logit * act.astype(F32)).reshape(64, 8, 256), axis=0)
        delta = (wl * d_logit * slope).astype(BF16).astype(F32)
        deltas.append(delta)
        scaled = (delta.reshape(64, 8, 256) * times.reshape(1, 8, 1)).reshape(512, 256)
        high = scaled.astype(BF16)
        low = scaled - high.astype(F32)
        parts.append(
            jnp.concatenate([scaled.T.astype(BF16), low.T.astype(BF16)], axis=0)
        )
    widen(wide_del, jnp.concatenate(deltas, axis=1))

    lane = lane_of((64, 128))
    is_low = lane < 64
    held_a = None
    for i in range(3):
        grad = None
        for half in range(2):
            term = dot(parts[half], rows_of(wide_act, half, i))
            grad = term if grad is None else grad + term
        grad = grad[:256] + grad[256:]
        for j in range(3):
            k = 3 * i + j
            g = [
                [grad[zo * 64 : zo * 64 + 64, j * 384 + p * 128 : j * 384 + p * 128 + 128] for p in range(3)]
                for zo in range(4)
            ]
            bc = g[0][0] + g[2][1]
            ab = g[1][0] + g[3][1]
            cb = pltpu.roll(bc, 64, 1)
            a_low = g[0][2] + pltpu.roll(g[2][0], 64, 1)
            ab = ab + jnp.where(is_low, a_low, cb)
            c_low = cb + g[1][1] + pltpu.roll(g[3][2], 64, 1)
            t = 3 * k // 2
            if k % 2 == 0:
                sums[t * 64 : t * 64 + 64, :] = ab
                held_a = c_low
            else:
                ba = pltpu.roll(ab, 64, 1)
                sums[t * 64 : t * 64 + 64, :] = jnp.where(is_low, held_a, ba)
                sums[(t + 1) * 64 : (t + 1) * 64 + 64, :] = jnp.where(
                    is_low, ba, pltpu.roll(c_low, 64, 1)
                )
    sums[13 * 64 : 14 * 64, :] = jnp.where(is_low, held_a, 0.0)

    firsts = []
    for half in range(2):
        d_act = None
        for i in range(3):
            term = dot(rows_of(wide_del, half, i), back[i])
            d_act = term if d_act is None else d_act + term
        d_first = (d_act * slope_one[:, half * 256 : half * 256 + 256]).astype(BF16).astype(F32)
        scaled = (d_first.reshape(64, 8, 256) * times.reshape(1, 8, 1)).reshape(512, 256)
        high = scaled.astype(BF16)
        low = scaled - high.astype(F32)
        firsts.append((scaled.T.astype(BF16), low.T.astype(BF16)))
    lhs = jnp.concatenate([firsts[0][0], firsts[1][0], firsts[0][1], firsts[1][1]], axis=0)
    packed = jnp.zeros((64, 128), F32)
    for i in range(3):
        grad = dot(lhs, first_in[i : i + 8].reshape(512, 128))
        grad = grad[:512] + grad[512:]
        total = None
        for zo in range(8):
            part = grad[zo * 64 : zo * 64 + 64]
            shift = (-3 * (zo - 1)) % 128
            part = pltpu.roll(part, shift, 1) if shift else part
            total = part if total is None else total + part
        for j in range(3):
            at = 9 * (3 * i + j)
            shift = (at - 32 * j) % 128
            moved = pltpu.roll(total, shift, 1) if shift else total
            packed = jnp.where((lane >= at) & (lane < at + 9), moved, packed)
    sums[896:960, :] = packed

    per_block = jnp.sum(loss, axis=1, keepdims=True) * (1.0 / (64 * 512))
    by_slot = jnp.sum(drawn * per_block, axis=0, keepdims=True)
    group = lax.axis_index("gy") * lax.axis_size("role") + lax.axis_index("role")
    row = lax.broadcasted_iota(jnp.int32, (16, 128), 0)
    spot = jnp.where(row % 2 == 0, by_slot[:, :128], by_slot[:, 128:])
    sums[960:976, :] = jnp.where(row // 2 == group, spot, 0.0)
    last = jnp.sum(last * times, axis=0, keepdims=True)
    last = last[:, :128] + last[:, 128:]
    last = last + pltpu.roll(last, 64, 1)
    sums[976:1024, :] = jnp.broadcast_to(last, (48, 128))

    lane = lane_of((64, 128))
    field = jnp.zeros((64, 128), F32)
    for half in range(2):
        for b in range(8):
            part = eddy_z[half, pl.ds(b, 64, stride=8), :]
            field = jnp.where(lane // 8 == 2 * b + half, part, field)
    field = 0.02 + field
    for x in range(8):
        rows = field[x * 8 : x * 8 + 8]
        for dx in range(2):
            visc[2 * x + dx, pl.ds(0, 8, stride=2), :] = rows
            visc[2 * x + dx, pl.ds(1, 8, stride=2), :] = rows


def local_part(velocity, target_visc, w_first, w_hidden, w_last, owner, block):
    consts = [jnp.asarray(a) for a in (pool_matrix(), target_matrix(), spread_matrix(), first_selector())]
    return pl.pallas_call(
        local_kernel,
        out_shape=(
            jax.ShapeDtypeStruct((1024, 128), F32),
            jax.ShapeDtypeStruct((16, 16, 128), F32),
        ),
        in_specs=[pl.BlockSpec(memory_space=pltpu.VMEM)] * 11,
        out_specs=(pl.BlockSpec(memory_space=pltpu.VMEM),) * 2,
        scratch_shapes=[
            pltpu.VMEM((512, 128), F32),
            pltpu.VMEM((10, 64, 128), BF16),
            pltpu.VMEM((3, 512, 128), BF16),
            pltpu.VMEM((3, 256, 1152), BF16),
            pltpu.VMEM((3, 1152, 256), BF16),
            pltpu.VMEM((2, 10, 64, 1152), BF16),
            pltpu.VMEM((2, 10, 64, 1152), BF16),
            pltpu.VMEM((512, 512), F32),
            pltpu.VMEM((8, 128), F32),
            pltpu.VMEM((2, 512, 128), F32),
        ],
        compiler_params=pltpu.CompilerParams(vmem_limit_bytes=48 * 1024 * 1024),
        name="local_part",
    )(
        velocity, target_visc, w_first, w_hidden, w_last.reshape(1, 64),
        owner.reshape(1, 256), block.reshape(1, 256), *consts,
    )

MESH = pl.DeviceIdType.MESH


def share_kernel(
    vel, visc, sums,
    u_next, slot_loss, grad_first, grad_hidden, grad_last,
    ext, y_out, y_in, z_out, z_in, half_in, half_sum, chunk_in, chunk_sum, deep_in, total,
    sems,
):
    gx, gy, role = lax.axis_index("gx"), lax.axis_index("gy"), lax.axis_index("role")
    depth, y = gx // 4, gx % 4
    x, core = (gy // 2) * 2 + role, gy % 2
    spot = y * 4 + x

    def plane(dy, dx):
        to_y, to_x = (y + dy) % 4, (x + dx) % 4
        return to_y * 4 + to_x, (depth * 4 + to_y, (to_x // 2) * 2 + core, to_x % 2)

    steps = [(dy, dx) for dy in range(4) for dx in range(4) if dy or dx]
    other = (gx, gy - core + 1 - core, role)
    x_up, x_down = ((gx + 1) % 32, gy, role), ((gx + 31) % 32, gy, role)
    y_up, y_down = (gx, (gy + 1) % 4, role), (gx, (gy + 3) % 4, role)
    z_side = (gx, gy, 1 - role)

    barrier = pltpu.get_barrier_semaphore()
    greeted = [plane(dy, dx)[1] for dy, dx in steps]
    greeted += [(((depth + d) % 8) * 4 + y, gy, role) for d in range(1, 8)]
    greeted += [x_up, x_down, y_up, y_down]
    for device in greeted:
        pl.semaphore_signal(barrier, inc=1, device_id=device, device_id_type=MESH)

    used = [0]

    def copy(src, dst, device):
        at = used[0]
        used[0] += 1
        return pltpu.make_async_remote_copy(
            src_ref=src, dst_ref=dst, send_sem=sems.at[0, at], recv_sem=sems.at[1, at],
            device_id=device, device_id_type=MESH,
        )

    for c in range(4):
        for h in range(1 if c == 3 else 2):
            for i in range(16):
                low = visc[i, 0:1, :] if c == 3 else vel[c, i, h : h + 1, :]
                high = visc[i, 15:16, :] if c == 3 else vel[c, i, 14 + h : 15 + h, :]
                y_out[0, 2 * c + h, i : i + 1, :] = low
                y_out[1, 2 * c + h, i : i + 1, :] = high
    lane = lane_of((16, 128))
    for c in range(4):
        for i in range(16):
            plane_of = visc[i] if c == 3 else vel[c, i]
            g = (c % 2) * 16 + i
            moved = pltpu.roll(plane_of, 2 + 4 * g, 1)
            if c % 2 == 0 and i == 0:
                packed = moved
            else:
                packed = jnp.where(lane // 4 == g, moved, packed)
            if c % 2 == 1 and i == 15:
                z_out[c // 2] = packed

    pl.semaphore_wait(barrier, len(greeted))

    first = copy(sums.at[pl.ds(pl.multiple_of((1 - core) * 512, 512), 512)], half_in, other)
    first.start()
    rims = [
        copy(vel.at[:, 0:2], ext.at[0:3, 18:20, 8:24], x_down),
        copy(vel.at[:, 14:16], ext.at[0:3, 0:2, 8:24], x_up),
        copy(visc.at[0:1], ext.at[3, 18:19, 8:24], x_down),
        copy(visc.at[15:16], ext.at[3, 1:2, 8:24], x_up),
        copy(y_out.at[0], y_in.at[1], y_down),
        copy(y_out.at[1], y_in.at[0], y_up),
        copy(z_out, z_in, z_side),
    ]
    for rim in rims:
        rim.start()
    for c in range(3):
        ext[c, 2:18, 8:24, :] = vel[c]
    ext[3, 2:18, 8:24, :] = visc[...]

    first.wait_recv()
    half_sum[...] = sums[pl.ds(pl.multiple_of(core * 512, 512), 512), :] + half_in[...]
    scatter = []
    for s, (dy, dx) in enumerate(steps):
        to, device = plane(dy, dx)
        scatter.append(
            copy(half_sum.at[pl.ds(pl.multiple_of(to * 32, 32), 32)], chunk_in.at[s], device)
        )
        scatter[-1].start()

    for rim in rims:
        rim.wait_recv()
    for c in range(4):
        for h in range(1 if c == 3 else 2):
            for i in range(16):
                at = 7 if c == 3 else 6 + h
                ext[c, 2 + i, at : at + 1, :] = y_in[0, 2 * c + h, i : i + 1, :]
                ext[c, 2 + i, 24 + h : 25 + h, :] = y_in[1, 2 * c + h, i : i + 1, :]

    def row(i, carry):
        def beside(c, here, far):
            turn = (254 - 4 * ((c % 2) * 16 + i)) % 128
            edge = pltpu.roll(z_in[c // 2], turn, 1)
            out = []
            for m in (1, 2) if far else (1,):
                after = jnp.where(lane < m, edge, here)
                before = jnp.where(lane >= 128 - m, edge, here)
                out += [pltpu.roll(after, 128 - m, 1), pltpu.roll(before, m, 1)]
            return out

        centre = ext[3, 2 + i, 8:24, :]
        sides = [
            (ext[3, 3 + i, 8:24, :], ext[3, 1 + i, 8:24, :]),
            (ext[3, 2 + i, 9:25, :], ext[3, 2 + i, 7:23, :]),
            beside(3, centre, False),
        ]
        sides = [(0.5 * (centre + a), 0.5 * (centre + b)) for a, b in sides]
        speed = [ext[c, 2 + i, 8:24, :] for c in range(3)]
        for c in range(3):
            here = speed[c]
            near = [
                [ext[c, 2 + i + m, 8:24, :] for m in (1, -1, 2, -2)],
                [ext[c, 2 + i, 8 + m : 24 + m, :] for m in (1, -1, 2, -2)],
                beside(c, here, True),
            ]
            change = None
            for axis in range(3):
                a1, b1, a2, b2 = near[axis]
                slope = (8.0 * (a1 - b1) - (a2 - b2)) * (1.0 / 12.0)
                term = sides[axis][0] * (a1 - here) - sides[axis][1] * (here - b1)
                term = term - speed[axis] * slope
                change = term if change is None else change + term
            u_next[c, i] = here + 0.2 * change
        return carry

    lax.fori_loop(0, 16, row, 0)

    for part in scatter:
        part.wait_recv()
    mine = half_sum[pl.ds(pl.multiple_of(spot * 32, 32), 32), :]
    for s in range(15):
        mine = mine + chunk_in[s]
    chunk_sum[...] = mine
    deep_in[depth] = mine
    deep = []
    for d in range(1, 8):
        device = (((depth + d) % 8) * 4 + y, gy, role)
        deep.append(copy(chunk_sum, deep_in.at[depth], device))
        deep[-1].start()
    for part in deep:
        part.wait_recv()
    mine = deep_in[0]
    for d in range(1, 8):
        mine = mine + deep_in[d]
    own = pl.ds(pl.multiple_of(core * 512 + spot * 32, 32), 32)
    total[own, :] = mine
    gather = []
    for s, (dy, dx) in enumerate(steps):
        device = plane(dy, dx)[1]
        gather.append(copy(total.at[own], total.at[own], device))
        gather[-1].start()
    across = []
    for dy in range(4):
        for part, (sy, _) in zip(gather, steps):
            if sy == dy:
                part.wait_recv()
        at = pl.ds(pl.multiple_of(core * 512 + ((y + 4 - dy) % 4) * 128, 128), 128)
        across.append(copy(total.at[at], total.at[at], other))
        across[-1].start()
    for part in across:
        part.wait_recv()

    for t in range(13):
        grad_hidden[:, t * 128 : (t + 1) * 128] = total[t * 64 : (t + 1) * 64, :]
    grad_hidden[:, 1664:1728] = total[832:896, :64]
    grad_first[...] = total[896:960, :81]
    grad_last[...] = total[976:977, :64]
    losses = total[960:976, :]
    at = lax.broadcasted_iota(jnp.int32, (16, 128), 0)
    losses = jnp.where(at == (gy * 2 + role) * 2 + gx // 16, losses, 0.0)
    losses = jnp.sum(losses, axis=0, keepdims=True)
    losses = pltpu.roll(losses, (128 - (gx % 16) * 8) % 128, 1)
    slot_loss[0] = losses[:, :8]
    for part in [first] + rims + scatter + deep + gather + across:
        part.wait_send()


COPIES = 1 + 7 + 15 + 7 + 15 + 4


def share_part(velocity, visc, sums):
    vmem = pl.BlockSpec(memory_space=pltpu.VMEM)
    return pl.pallas_call(
        share_kernel,
        out_shape=(
            jax.ShapeDtypeStruct((3, 16, 16, 128), F32),
            jax.ShapeDtypeStruct((1, 1, 8), F32),
            jax.ShapeDtypeStruct((64, 81), F32),
            jax.ShapeDtypeStruct((64, 1728), F32),
            jax.ShapeDtypeStruct((1, 64), F32),
        ),
        in_specs=[vmem] * 3,
        out_specs=(vmem,) * 5,
        scratch_shapes=[
            pltpu.VMEM((4, 20, 32, 128), F32),
            pltpu.VMEM((2, 7, 16, 128), F32),
            pltpu.VMEM((2, 7, 16, 128), F32),
            pltpu.VMEM((2, 16, 128), F32),
            pltpu.VMEM((2, 16, 128), F32),
            pltpu.VMEM((512, 128), F32),
            pltpu.VMEM((512, 128), F32),
            pltpu.VMEM((15, 32, 128), F32),
            pltpu.VMEM((32, 128), F32),
            pltpu.VMEM((8, 32, 128), F32),
            pltpu.VMEM((1024, 128), F32),
            pltpu.SemaphoreType.DMA((2, COPIES)),
        ],
        compiler_params=pltpu.CompilerParams(
            vmem_limit_bytes=48 * 1024 * 1024, collective_id=0, has_side_effects=True
        ),
        name="share_part",
    )(velocity, visc, sums)


def on_device(velocity, target_visc, w_first, w_hidden, w_last, sample_owner, sample_block):
    sums, visc = local_part(
        velocity, target_visc, w_first, w_hidden, w_last, sample_owner, sample_block
    )
    u_next, slot_loss, grad_first, grad_hidden, grad_last = share_part(velocity, visc, sums)
    return (u_next, slot_loss, grad_first, grad_hidden, grad_last.reshape(64))


def solution(mesh):
    return jax.shard_map(
        on_device,
        mesh=mesh,
        in_specs=(
            P(None, "gx", "gy", "role"),
            P("gx", "gy", "role"),
            P(),
            P(),
            P(),
            P("gy", "role", None, None),
            P("gy", "role", None, None),
        ),
        out_specs=(P(None, "gx", "gy", "role"), P("gy", "role", "gx"), P(), P(), P()),
        check_vma=False,
    )
```

time: 475 us -> 60.5 us (0.13)
  waiting for transfers between devices: 176 us -> 0 us
  matrix products: 86.1 us -> 0 us
  blocking collectives: 74.4 us -> 0 us
  local copies, waits for them, and re-layouts: 63.8 us -> 10.8 us
  Pallas kernels: 0 us -> 48.5 us
  other arithmetic: 30.2 us -> 0 us
  starting transfers between devices: 24.2 us -> 0 us
  between operations: 16.6 us -> 0.68 us
    psum x1 -> x0, waiting for transfers between devices: 171 us -> none  [on_device(): lax.psum((grad_first, grad_hidden, grad_last), ('gx', 'gy', 'role'))]
    dot_general x192 -> x0, matrix products: 86.1 us -> none  [the longest x107 49.1 us: convolve(): jnp.einsum('oc,bcn->bon', weight[:, k * inner:(k + 1) * inner], shifted(p...]
    psum x1 -> x0, blocking collectives: 74.4 us -> none  [on_device(): lax.psum((grad_first, grad_hidden, grad_last), ('gx', 'gy', 'role'))]
    pallas_call x0 -> x2, Pallas kernels: none -> 48.5 us  [the longest x1 33.8 us: share_part(): pl.pallas_call(share_kernel, out_shape=(jax.ShapeDtypeStruct((3, 16, 16,...]
    reshape x11 -> x0, local copies, waits for them, and re-layouts: 31.1 us -> none  [the longest x1 27.3 us: on_device(): velocity.reshape(3, half_x, 2, half_y, 2, half_z, 2).mean(axis=(2, 4, 6))]
    ppermute x12 -> x0, starting transfers between devices: 23.6 us -> none  [the longest x6 13.2 us: padded_2(): lax.ppermute(lax.slice_in_dim(block, 0, width, axis=dim), axis, backward)]
    ppermute x6 -> x0, local copies, waits for them, and re-layouts: 11.6 us -> none  [the longest x3 6.22 us: padded_2(): lax.ppermute(lax.slice_in_dim(block, block.shape[dim] - width, None, axis...]
    concatenate x6 -> x0, local copies, waits for them, and re-layouts: 10 us -> none  [the longest x4 8.34 us: padded_2(): block = jnp.concatenate([low, block, high], axis=dim)]
  transfers between devices with their start and end apart: 14 -> 0, of which waited for: 4 -> 0; matrix products, arithmetic and copies ran while one was open for 17% -> 0% of each run, Pallas kernels for 0% -> 0%
where the time goes in v1:
time: 60.5 us; the launch traced here: 60 us
  Pallas kernels  48.5 us (80%)
  local copies, waits for them, and re-layouts  10.8 us (18%)
  between operations  0.68 us (1%)
    pallas_call x1, Pallas kernels, share_part(): pl.pallas_call(share_kernel, out_shape=(jax.ShapeDtypeStruct((3, 16, 16,...  33.8 us
    pallas_call x1, Pallas kernels, local_part(): pl.pallas_call(local_kernel, out_shape=(jax.ShapeDtypeStruct((1024, 128),...  14.8 us
    unnamed x27, local copies, waits for them, and re-layouts  10.8 us

profile of v1, /device:TPU:1, one launch (start us, length us, event | category | flops | bytes accessed | tf_op | source)
XLA Modules:
  0.0 60.0 jit_solution(3071212048698717625)
XLA Ops:
  0.6 0.0 copy-start.9
  0.6 0.0 copy-start.8
  0.7 0.0 copy-start.10
  0.7 0.7 %copy-done.9 = s32[1,1,256,1]{2,3,1,0:T(1,128)S(1)} copy-done((s32[1,1,256,1]{2,3,1,0:T(1,128)S(1)}, s32[1,1,256,1]{2,3,1,0:T(1,128)}, u32[]{:S(2)}) %copy-start.9) | copy-done | bytes 1048
  1.3 0.0 copy-done.8
  1.3 0.0 copy-done.10
  1.3 0.0 copy-start
  1.3 1.0 %copy-done = f32[3,16,16,128]{3,2,1,0:T(8,128)S(1)} copy-done((f32[3,16,16,128]{3,2,1,0:T(8,128)S(1)}, f32[3,16,16,128]{3,2,1,0:T(8,128)}, u32[]{:S(2)}) %copy-start) | copy-done | bytes 393240
  2.3 0.0 copy-start.1
  2.3 1.0 %copy-done.1 = bf16[81,3072]{1,0:T(8,128)(2,1)S(1)} copy-done((bf16[81,3072]{1,0:T(8,128)(2,1)S(1)}, bf16[81,3072]{1,0:T(8,128)(2,1)}, u32[]{:S(2)}) %copy-start.1) | copy-done | bytes 497688
  3.4 0.0 copy-start.2
  3.4 0.9 %copy-done.2 = bf16[64,1728]{1,0:T(8,128)(2,1)S(1)} copy-done((bf16[64,1728]{1,0:T(8,128)(2,1)S(1)}, bf16[64,1728]{1,0:T(8,128)(2,1)}, u32[]{:S(2)}) %copy-start.2) | copy-done | bytes 221208
  4.3 0.0 copy-start.3
  4.3 0.9 %copy-done.3 = bf16[384,256]{1,0:T(8,128)(2,1)S(1)} copy-done((bf16[384,256]{1,0:T(8,128)(2,1)S(1)}, bf16[384,256]{1,0:T(8,128)(2,1)}, u32[]{:S(2)}) %copy-start.3) | copy-done | bytes 196632
  5.2 0.0 copy-start.4
  5.2 0.9 %copy-done.4 = bf16[128,512]{1,0:T(8,128)(2,1)S(1)} copy-done((bf16[128,512]{1,0:T(8,128)(2,1)S(1)}, bf16[128,512]{1,0:T(8,128)(2,1)}, u32[]{:S(2)}) %copy-start.4) | copy-done | bytes 131096
  6.1 0.0 copy-start.5
  6.2 0.8 %copy-done.5 = bf16[64,256]{1,0:T(8,128)(2,1)S(1)} copy-done((bf16[64,256]{1,0:T(8,128)(2,1)S(1)}, bf16[64,256]{1,0:T(8,128)(2,1)}, u32[]{:S(2)}) %copy-start.5) | copy-done | bytes 32792
  6.9 0.0 copy-start.6
  6.9 0.7 %copy-done.6 = bf16[8,8,64]{2,1,0:T(8,128)(2,1)S(1)} copy-done((bf16[8,8,64]{2,1,0:T(8,128)(2,1)S(1)}, bf16[8,8,64]{2,1,0:T(8,128)(2,1)}, u32[]{:S(2)}) %copy-start.6) | copy-done | bytes 8216
  7.6 0.0 copy-start.7
  7.6 0.7 %copy-done.7 = bf16[64,81]{1,0:T(8,128)(2,1)S(1)} copy-done((bf16[64,81]{1,0:T(8,128)(2,1)S(1)}, bf16[64,81]{1,0:T(8,128)(2,1)}, u32[]{:S(2)}) %copy-start.7) | copy-done | bytes 10392
  8.3 14.8 %local_part.1 = (f32[1024,128]{1,0:T(8,128)S(1)}, f32[16,16,128]{2,1,0:T(8,128)S(1)}) custom-call(f32[3,16,16,128]{3,2,1,0:T(8,128)S(1)} %copy-done, bf16[8,8,64]{2,1,0:T(8,128)(2,1)S(1)} %copy-done.6, bf16[64,81]{1,0:T(8,128)(2,1)S(1)} %copy-done.7, bf16[64,1728]{1,0:T(8,128)(2,1)S(1)} %copy-done.2, bf16[1,64]{1,0:T(2,128)(2,1)S(1)} %bitcast.6, ...), custom_call_target="tpu_custom_call" | custom-call | tf_op jit(solution)/shard_map/local_part/pallas_call | solution.py:320
  23.1 33.8 %share_part.1 = (f32[3,16,16,128]{3,2,1,0:T(8,128)S(1)}, f32[1,1,8]{2,1,0:T(1,128)S(1)}, f32[64,81]{1,0:T(8,128)S(1)}, f32[64,1728]{1,0:T(8,128)S(1)}, f32[1,64]{1,0:T(1,128)S(1)}) custom-call(f32[3,16,16,128]{3,2,1,0:T(8,128)S(1)} %copy-done, f32[16,16,128]{2,1,0:T(8,128)S(1)} %get-tuple-element.12.visc, f32[1024,128]{1,0:T(8,128)S(1)} %get-tuple-element.13.sums), custom_call_target="tpu_custom_call" | custom-call | tf_op jit(solution)/shard_map/share_part/pallas_call | solution.py:539
  56.9 0.7 %copy.21 = f32[3,16,16,128]{3,2,1,0:T(8,128)} copy(f32[3,16,16,128]{3,2,1,0:T(8,128)S(1)} %get-tuple-element.24) | data formatting | bytes 786432
  57.6 0.5 copy.22
  58.1 0.6 %copy.23 = f32[64,81]{1,0:T(8,128)} copy(f32[64,81]{1,0:T(8,128)S(1)} %get-tuple-element.26) | data formatting | bytes 41472
  58.8 0.8 %copy.24 = f32[64,1728]{1,0:T(8,128)} copy(f32[64,1728]{1,0:T(8,128)S(1)} %get-tuple-element.27) | data formatting | bytes 884736
  59.5 0.5 copy.25
Async XLA Ops:
  0.6 0.7 %copy-start.9 = (s32[1,1,256,1]{2,3,1,0:T(1,128)S(1)}, s32[1,1,256,1]{2,3,1,0:T(1,128)}, u32[]{:S(2)}) copy-start(s32[1,1,256,1]{2,3,1,0:T(1,128)} %param.17) | copy-start | bytes 3076
  0.6 0.7 %copy-start.8 = (s32[1,1,256,1]{2,3,1,0:T(1,128)S(1)}, s32[1,1,256,1]{2,3,1,0:T(1,128)}, u32[]{:S(2)}) copy-start(s32[1,1,256,1]{2,3,1,0:T(1,128)} %param.16) | copy-start | bytes 3076
  0.7 0.7 %copy-start.10 = (bf16[64]{0:T(256)(128)(2,1)S(1)}, bf16[64]{0:T(256)(128)(2,1)}, u32[]{:S(2)}) copy-start(bf16[64]{0:T(256)(128)(2,1)} %param.15) | copy-start | bytes 388
  1.3 1.0 %copy-start = (f32[3,16,16,128]{3,2,1,0:T(8,128)S(1)}, f32[3,16,16,128]{3,2,1,0:T(8,128)}, u32[]{:S(2)}) copy-start(f32[3,16,16,128]{3,2,1,0:T(8,128)} %vel.3) | copy-start | bytes 1179652
  2.3 1.0 %copy-start.1 = (bf16[81,3072]{1,0:T(8,128)(2,1)S(1)}, bf16[81,3072]{1,0:T(8,128)(2,1)}, u32[]{:S(2)}) copy-start(bf16[81,3072]{1,0:T(8,128)(2,1)} %constant.11.clone.sel) | copy-start | bytes 1492996
  3.4 0.9 %copy-start.2 = (bf16[64,1728]{1,0:T(8,128)(2,1)S(1)}, bf16[64,1728]{1,0:T(8,128)(2,1)}, u32[]{:S(2)}) copy-start(bf16[64,1728]{1,0:T(8,128)(2,1)} %w_hidden.1) | copy-start | bytes 663556
  4.3 0.9 %copy-start.3 = (bf16[384,256]{1,0:T(8,128)(2,1)S(1)}, bf16[384,256]{1,0:T(8,128)(2,1)}, u32[]{:S(2)}) copy-start(bf16[384,256]{1,0:T(8,128)(2,1)} %constant.8.clone.pool) | copy-start | bytes 589828
  5.2 0.9 %copy-start.4 = (bf16[128,512]{1,0:T(8,128)(2,1)S(1)}, bf16[128,512]{1,0:T(8,128)(2,1)}, u32[]{:S(2)}) copy-start(bf16[128,512]{1,0:T(8,128)(2,1)} %constant.10.clone.spread) | copy-start | bytes 393220
  6.1 0.8 %copy-start.5 = (bf16[64,256]{1,0:T(8,128)(2,1)S(1)}, bf16[64,256]{1,0:T(8,128)(2,1)}, u32[]{:S(2)}) copy-start(bf16[64,256]{1,0:T(8,128)(2,1)} %constant.9.clone.tmat) | copy-start | bytes 98308
  6.9 0.7 %copy-start.6 = (bf16[8,8,64]{2,1,0:T(8,128)(2,1)S(1)}, bf16[8,8,64]{2,1,0:T(8,128)(2,1)}, u32[]{:S(2)}) copy-start(bf16[8,8,64]{2,1,0:T(8,128)(2,1)} %target.1) | copy-start | bytes 24580
  7.6 0.7 %copy-start.7 = (bf16[64,81]{1,0:T(8,128)(2,1)S(1)}, bf16[64,81]{1,0:T(8,128)(2,1)}, u32[]{:S(2)}) copy-start(bf16[64,81]{1,0:T(8,128)(2,1)} %w_first.1) | copy-start | bytes 31108

commit v2 on v1

v2 whole, which is shorter than its diff:
```python
import numpy as np
import jax
import jax.numpy as jnp
from jax import lax
from jax.sharding import PartitionSpec as P
from jax.experimental import pallas as pl
from jax.experimental.pallas import tpu as pltpu

SIDE = 8
CH = 64
F32 = jnp.float32
BF16 = jnp.bfloat16
NT = (((1,), (1,)), ((), ()))
NN = (((1,), (0,)), ((), ()))
MESH = pl.DeviceIdType.MESH


def dot(a, b, dims=NN):
    return lax.dot_general(a, b, dims, preferred_element_type=F32)


def pool_matrix():
    z = np.arange(128)[:, None]
    lane = np.arange(256)[None, :]
    block, inner = lane // 32, lane % 32
    parts = []
    for comp in range(3):
        hit = (inner < 24) & (inner % 3 == comp) & (z // 2 == block * 8 + inner // 3)
        parts.append(np.where(hit, 0.125, 0.0))
    return np.concatenate(parts, 0).astype(jnp.bfloat16)


def target_matrix():
    z = np.arange(64)[:, None]
    lane = np.arange(256)[None, :]
    block, inner = lane // 32, lane % 32
    return ((inner >= 24) & (z == block * 8 + inner - 24)).astype(jnp.bfloat16)


def spread_matrix():
    row = np.arange(128)[:, None]
    lane = np.arange(512)[None, :]
    return (row == 24 + lane // 64).astype(jnp.bfloat16)


def first_selector():
    out = np.zeros((81, 3, 8, 128), np.float32)
    for i in range(3):
        for zo in range(8):
            for j in range(3):
                for t in range(9):
                    zi = zo - 1 + t // 3
                    if 0 <= zi < 8:
                        out[9 * (3 * i + j) + t, i, zo, j * 32 + zi * 3 + t % 3] = 1.0
    return out.reshape(81, 3072).astype(jnp.bfloat16)


def lane_of(shape):
    return lax.broadcasted_iota(jnp.int32, shape, len(shape) - 1)


def shift_y(field, shift):
    zero = jnp.zeros((8, 8, field.shape[2]), field.dtype)
    if shift < 0:
        return jnp.concatenate([zero, field[:, :56]], axis=1)
    if shift > 0:
        return jnp.concatenate([field[:, 8:], zero], axis=1)
    return field


def widen(store, field):
    lane = lane_of((512, 128))
    zero = jnp.zeros((64, 1152), BF16)
    near = [
        jnp.where(lane >= 64, pltpu.roll(field[:, 256:384], 64, 1), 0.0),
        jnp.where(lane < 64, pltpu.roll(field[:, 128:256], 64, 1), 0.0),
    ]
    for half in range(2):
        store[half, 0] = zero
        store[half, 9] = zero
        whole = jnp.concatenate([field[:, half * 256 : half * 256 + 256], near[half]], axis=1)
        whole = whole.reshape(8, 64, 384)
        for j in range(3):
            store[half, 1:9, :, j * 384 : (j + 1) * 384] = shift_y(whole, j - 1).astype(BF16)


def rows_of(store, half, i):
    return store[half, i : i + 8].reshape(512, 1152)


def place_weights(w_hidden, ahead, back):
    lane = lane_of((64, 128))
    low = lane < 64
    zero = jnp.zeros((64, 128), BF16)
    tiles = [w_hidden[:, t * 128 : (t + 1) * 128] for t in range(13)]
    last = w_hidden[:, 1664:1728]
    tiles.append(jnp.concatenate([last, last], axis=1))
    tiles = [t.astype(F32) for t in tiles]
    swapped = [pltpu.roll(t, 64, 1) for t in tiles]
    for j in range(9):
        t = 3 * j // 2
        if j % 2 == 0:
            ab = tiles[t]
            bc = jnp.where(low, swapped[t], swapped[t + 1])
            c_low, c_high = tiles[t + 1], swapped[t + 1]
            a_low, a_high = tiles[t], swapped[t]
        else:
            bc = tiles[t + 1]
            ab = jnp.where(low, swapped[t], swapped[t + 1])
            c_low, c_high = swapped[t + 1], tiles[t + 1]
            a_low, a_high = swapped[t], tiles[t]
        c_0 = jnp.where(low, c_low, 0.0).astype(BF16)
        o_c = jnp.where(low, 0.0, c_high).astype(BF16)
        a_0 = jnp.where(low, a_low, 0.0).astype(BF16)
        o_a = jnp.where(low, 0.0, a_high).astype(BF16)
        ab = ab.astype(BF16)
        bc = bc.astype(BF16)
        rows = [(bc, zero, a_0), (ab, c_0, zero), (o_a, bc, zero), (zero, ab, o_c)]
        for zo in range(4):
            for part in range(3):
                start = (j % 3) * 384 + part * 128
                ahead[j // 3, zo * 64 : (zo + 1) * 64, start : start + 128] = rows[zo][part]
        flip = 8 - j
        rows = [(bc, zero), (ab, c_0), (o_a, bc), (zero, ab), (c_0, zero), (zero, o_a)]
        for zi in range(6):
            start = (flip % 3) * 384 + zi * 64
            for part in range(2):
                back[flip // 3, start : start + 64, part * 128 : (part + 1) * 128] = rows[zi][part]


def whole_kernel(*refs):
    sources, refs = refs[:9], refs[9:]
    (u_next, slot_loss, grad_first, grad_hidden, grad_last), refs = refs[:5], refs[5:]
    held_in, refs = refs[:9], refs[9:]
    vel, target, w_first, w_hidden, w_last, owner, block, fixed, sel = held_in
    (
        filt, first_in, w_one, ahead, back, wide_act, wide_del, slope_one, eddy_z,
        sums, first_sums, ext, y_out, y_in, z_out, z_in,
        half_in, half_sum, chunk_in, chunk_sum, deep_in, total,
        f_in, f_sum, f_plane, f_mid, f_deep, f_total,
        local_sems, sems,
    ) = refs

    loads = [
        pltpu.make_async_copy(src, dst, local_sems.at[n])
        for n, (src, dst) in enumerate(zip(sources, held_in))
    ]
    for n in (3, 0, 2, 8, 7, 1, 4, 5, 6):
        loads[n].start()

    gx, gy, role = lax.axis_index("gx"), lax.axis_index("gy"), lax.axis_index("role")
    depth, y = gx // 4, gx % 4
    x, core = (gy // 2) * 2 + role, gy % 2
    spot = y * 4 + x

    def plane(dy, dx):
        to_y, to_x = (y + dy) % 4, (x + dx) % 4
        return to_y * 4 + to_x, (depth * 4 + to_y, (to_x // 2) * 2 + core, to_x % 2)

    steps = [(dy, dx) for dy in range(4) for dx in range(4) if dy or dx]
    deeper = [(((depth + d) % 8) * 4 + y, gy, role) for d in range(1, 8)]
    other = (gx, gy - core + 1 - core, role)
    x_up, x_down = ((gx + 1) % 32, gy, role), ((gx + 31) % 32, gy, role)
    y_up, y_down = (gx, (gy + 1) % 4, role), (gx, (gy + 3) % 4, role)
    z_side = (gx, gy, 1 - role)

    barrier = pltpu.get_barrier_semaphore()
    greeted = [plane(dy, dx)[1] for dy, dx in steps] + deeper + [x_up, x_down, y_up, y_down]
    for device in greeted:
        pl.semaphore_signal(barrier, inc=1, device_id=device, device_id_type=MESH)

    started = []

    def send(src, dst, device):
        at = len(started)
        part = pltpu.make_async_remote_copy(
            src_ref=src, dst_ref=dst, send_sem=sems.at[0, at], recv_sem=sems.at[1, at],
            device_id=device, device_id_type=MESH,
        )
        started.append(part)
        part.start()
        return part

    loads[3].wait()
    place_weights(w_hidden, ahead, back)
    loads[2].wait()
    loads[8].wait()
    placed = dot(w_first[...], sel[...]).astype(BF16)
    for i in range(3):
        for zo in range(8):
            at = (i * 8 + zo) * 128
            w_one[i, zo * 64 : (zo + 1) * 64, :] = placed[:, at : at + 128]

    for n in (0, 7, 1, 4, 5, 6):
        loads[n].wait()
    pooled = []
    for comp in range(3):
        summed = None
        for dx in range(2):
            for dy in range(2):
                part = jnp.concatenate(
                    [vel[comp, 2 * i + dx, pl.ds(dy, 8, stride=2), :] for i in range(8)], axis=0
                )
                summed = part if summed is None else summed + part
        pooled.append(summed)
    rest = jnp.concatenate(pooled, axis=1)
    blocks = None
    for _ in range(3):
        piece = rest.astype(BF16)
        rest = rest - piece.astype(F32)
        term = dot(piece, fixed[0:384])
        blocks = term if blocks is None else blocks + term
    blocks = blocks.astype(BF16).astype(F32)
    want = target[...].astype(F32).reshape(64, 64).astype(BF16)
    blocks = blocks + dot(want, fixed[384:448])
    for b in range(8):
        tile = blocks[:, (b // 4) * 128 : (b // 4) * 128 + 128]
        if b % 4:
            tile = pltpu.roll(tile, 128 - 32 * (b % 4), 1)
        filt[pl.ds(b, 64, stride=8), :] = tile
    held = filt[...]
    held16 = held.astype(BF16)
    targets = jnp.concatenate([dot(held16, fixed[448:576]), dot(held16, fixed[576:704])], axis=1)
    lane = lane_of((512, 128))
    inputs = jnp.where(lane < 24, held, 0.0).reshape(8, 64, 128)
    near = shift_y(inputs, -1)
    near = near + pltpu.roll(inputs.reshape(512, 128), 32, 1).reshape(8, 64, 128)
    near = near + pltpu.roll(shift_y(inputs, 1).reshape(512, 128), 64, 1).reshape(8, 64, 128)
    first_in[0] = jnp.zeros((64, 128), BF16)
    first_in[9] = jnp.zeros((64, 128), BF16)
    first_in[1:9] = near.astype(BF16)

    pre = None
    for i in range(3):
        term = dot(first_in[i : i + 8].reshape(512, 128), w_one[i], NT)
        pre = term if pre is None else pre + term
    sig = 1.0 / (1.0 + jnp.exp(-pre))
    slope_one[...] = sig * (1.0 + pre * (1.0 - sig))
    widen(wide_act, (pre * sig).astype(BF16).astype(F32))

    slot_of, base_of = (0, 0, 1, 2), (0, 16, 0, 0)
    lane16 = lane_of((16, 128))

    def pack_sides(c, field, wide):
        for h in range(wide):
            for i in range(16):
                low, high = field[i, h : h + 1, :], field[i, 16 - wide + h : 17 - wide + h, :]
                y_out[0, 2 * c + h, i : i + 1, :] = low
                y_out[1, 2 * c + h, i : i + 1, :] = high
        packed = None
        for i in range(16):
            g = base_of[c] + i
            moved = pltpu.roll(field[i], 2 + 4 * g, 1)
            packed = moved if packed is None else jnp.where(lane16 // 4 == g, moved, packed)
        return packed

    sides_of = [pack_sides(c, vel.at[c], 2) for c in range(3)]
    z_out[0] = jnp.where(lane16 < 64, sides_of[0], sides_of[1])
    z_out[1] = sides_of[2]

    wl = w_last[...].astype(F32)
    wl = jnp.concatenate([wl, wl, wl, wl], axis=1)
    rows_iota = lax.broadcasted_iota(jnp.int32, (384, 256), 0)
    lanes_iota = lax.broadcasted_iota(jnp.int32, (384, 256), 1)
    cell = jnp.where(rows_iota < 256, rows_iota // 64, (rows_iota // 2) % 4)
    out_map = jnp.where(cell == lanes_iota // 64, wl, 0.0).astype(BF16)

    number = lax.broadcasted_iota(jnp.int32, (8, 256), 0)
    drawn = jnp.where((owner[...] == gx) & (block[...] == number), 1.0, 0.0)
    times = jnp.sum(drawn, axis=1, keepdims=True)

    loss = jnp.zeros((8, 256), F32)
    last = jnp.zeros((8, 256), F32)
    deltas, parts = [], []
    for half in range(2):
        pre = None
        for i in range(3):
            term = dot(rows_of(wide_act, half, i), ahead[i], NT)
            pre = term if pre is None else pre + term
        sig = 1.0 / (1.0 + jnp.exp(-pre))
        act = (pre * sig).astype(BF16)
        slope = sig * (1.0 + pre * (1.0 - sig))
        both = dot(act, out_map, NT)
        logits = both[:, :256]
        eddy_z[half] = 0.5 * (
            jnp.maximum(both[:, 256:], 0.0) + jnp.log1p(jnp.exp(-jnp.abs(both[:, 256:])))
        )
        small = jnp.exp(-jnp.abs(logits))
        eddy = 0.5 * (jnp.maximum(logits, 0.0) + jnp.log1p(small))
        gate = jnp.where(logits >= 0, 1.0, small) / (1.0 + small)
        error = eddy - targets[:, half * 256 : half * 256 + 256]
        loss = loss + jnp.sum((error * error).reshape(64, 8, 256), axis=0)
        d_logit = (error * gate * (1.0 / (256 * 512))).astype(BF16).astype(F32)
        last = last + jnp.sum((d_logit * act.astype(F32)).reshape(64, 8, 256), axis=0)
        delta = (wl * d_logit * slope).astype(BF16).astype(F32)
        deltas.append(delta)
        scaled = (delta.reshape(64, 8, 256) * times.reshape(1, 8, 1)).reshape(512, 256)
        low = scaled - scaled.astype(BF16).astype(F32)
        parts.append(jnp.concatenate([scaled.T.astype(BF16), low.T.astype(BF16)], axis=0))
    widen(wide_del, jnp.concatenate(deltas, axis=1))

    lane = lane_of((64, 128))
    field = jnp.zeros((64, 128), F32)
    for half in range(2):
        for b in range(8):
            part = eddy_z[half, pl.ds(b, 64, stride=8), :]
            field = jnp.where(lane // 8 == 2 * b + half, part, field)
    field = 0.02 + field
    for i in range(8):
        for dx in range(2):
            for dy in range(2):
                ext[3, 2 + 2 * i + dx, pl.ds(8 + dy, 8, stride=2), :] = field[i * 8 : i * 8 + 8]
    z_out[2] = pack_sides(3, ext.at[3, 2:18, 8:24], 1)
    pl.semaphore_wait(barrier, len(greeted))
    rims = [
        send(vel.at[:, 0:2], ext.at[0:3, 18:20, 8:24], x_down),
        send(vel.at[:, 14:16], ext.at[0:3, 0:2, 8:24], x_up),
        send(ext.at[3, 2:3, 8:24], ext.at[3, 18:19, 8:24], x_down),
        send(ext.at[3, 17:18, 8:24], ext.at[3, 1:2, 8:24], x_up),
        send(y_out.at[0], y_in.at[1], y_down),
        send(y_out.at[1], y_in.at[0], y_up),
        send(z_out, z_in, z_side),
    ]

    per_block = jnp.sum(loss, axis=1, keepdims=True) * (1.0 / (64 * 512))
    by_slot = jnp.sum(drawn * per_block, axis=0, keepdims=True)
    group = gy * 2 + role
    at = lax.broadcasted_iota(jnp.int32, (64, 128), 0)
    by_slot = jnp.where(at % 2 == 0, by_slot[:, :128], by_slot[:, 128:])
    sums[0, 448:512, :] = jnp.where(at // 2 == group, by_slot, 0.0)
    last = jnp.sum(last * times, axis=0, keepdims=True)
    last = last[:, :128] + last[:, 128:]
    last = last + pltpu.roll(last, 64, 1)
    sums[1, 448:512, :] = jnp.broadcast_to(last, (64, 128))

    def column(t, value):
        sums[t // 7, (t % 7) * 64 : (t % 7) * 64 + 64, :] = value

    is_low = lane < 64
    held_a = None
    for i in range(3):
        grad = None
        for half in range(2):
            term = dot(parts[half], rows_of(wide_act, half, i))
            grad = term if grad is None else grad + term
        grad = grad[:256] + grad[256:]
        for j in range(3):
            k = 3 * i + j
            g = [
                [grad[zo * 64 : zo * 64 + 64, j * 384 + p * 128 : j * 384 + p * 128 + 128] for p in range(3)]
                for zo in range(4)
            ]
            bc = g[0][0] + g[2][1]
            ab = g[1][0] + g[3][1]
            cb = pltpu.roll(bc, 64, 1)
            a_low = g[0][2] + pltpu.roll(g[2][0], 64, 1)
            ab = ab + jnp.where(is_low, a_low, cb)
            c_low = cb + g[1][1] + pltpu.roll(g[3][2], 64, 1)
            t = 3 * k // 2
            if k % 2 == 0:
                column(t, ab)
                held_a = c_low
            else:
                ba = pltpu.roll(ab, 64, 1)
                column(t, jnp.where(is_low, held_a, ba))
                column(t + 1, jnp.where(is_low, ba, pltpu.roll(c_low, 64, 1)))
    column(13, jnp.where(is_low, held_a, 0.0))
    first = send(sums.at[1 - core], half_in, other)

    firsts = []
    scatter = []
    for half in range(2):
        d_act = None
        for i in range(3):
            term = dot(rows_of(wide_del, half, i), back[i])
            d_act = term if d_act is None else d_act + term
        d_first = (d_act * slope_one[:, half * 256 : half * 256 + 256]).astype(BF16).astype(F32)
        scaled = (d_first.reshape(64, 8, 256) * times.reshape(1, 8, 1)).reshape(512, 256)
        low = scaled - scaled.astype(BF16).astype(F32)
        firsts.append((scaled.T.astype(BF16), low.T.astype(BF16)))
        if half == 0:
            first.wait_recv()
            half_sum[...] = sums[core] + half_in[...]
            for s, (dy, dx) in enumerate(steps):
                to, device = plane(dy, dx)
                scatter.append(
                    send(half_sum.at[pl.ds(pl.multiple_of(to * 32, 32), 32)], chunk_in.at[s], device)
                )
    lhs = jnp.concatenate([firsts[0][0], firsts[1][0], firsts[0][1], firsts[1][1]], axis=0)
    packed = jnp.zeros((64, 128), F32)
    for i in range(3):
        grad = dot(lhs, first_in[i : i + 8].reshape(512, 128))
        grad = grad[:512] + grad[512:]
        summed = None
        for zo in range(8):
            part = grad[zo * 64 : zo * 64 + 64]
            shift = (-3 * (zo - 1)) % 128
            part = pltpu.roll(part, shift, 1) if shift else part
            summed = part if summed is None else summed + part
        for j in range(3):
            start = 9 * (3 * i + j)
            shift = (start - 32 * j) % 128
            moved = pltpu.roll(summed, shift, 1) if shift else summed
            packed = jnp.where((lane >= start) & (lane < start + 9), moved, packed)
    first_sums[...] = packed

    own32 = pl.ds(pl.multiple_of(core * 32, 32), 32)
    f_first = send(
        first_sums.at[pl.ds(pl.multiple_of((1 - core) * 32, 32), 32)], f_in, other
    )
    ext[0:3, 2:18, 8:24, :] = vel[...]
    f_first.wait_recv()
    mine = first_sums[own32, :] + f_in[...]
    f_sum[...] = mine
    f_plane[spot] = mine
    f_across = [send(f_sum, f_plane.at[spot], plane(dy, dx)[1]) for dy, dx in steps]

    for part in scatter:
        part.wait_recv()
    mine = half_sum[pl.ds(pl.multiple_of(spot * 32, 32), 32), :]
    for s in range(15):
        mine = mine + chunk_in[s]
    chunk_sum[...] = mine
    deep_in[depth] = mine
    deep = [send(chunk_sum, deep_in.at[depth], device) for device in deeper]

    for rim in rims:
        rim.wait_recv()
    for c in range(4):
        for h in range(1 if c == 3 else 2):
            for i in range(16):
                to = 7 if c == 3 else 6 + h
                ext[c, 2 + i, to : to + 1, :] = y_in[0, 2 * c + h, i : i + 1, :]
                ext[c, 2 + i, 24 + h : 25 + h, :] = y_in[1, 2 * c + h, i : i + 1, :]

    def row(i, carry):
        def beside(c, here, far):
            turn = (254 - 4 * (base_of[c] + i)) % 128
            edge = pltpu.roll(z_in[slot_of[c]], turn, 1)
            out = []
            for m in (1, 2) if far else (1,):
                after = jnp.where(lane16 < m, edge, here)
                before = jnp.where(lane16 >= 128 - m, edge, here)
                out += [pltpu.roll(after, 128 - m, 1), pltpu.roll(before, m, 1)]
            return out

        centre = ext[3, 2 + i, 8:24, :]
        sides = [
            (ext[3, 3 + i, 8:24, :], ext[3, 1 + i, 8:24, :]),
            (ext[3, 2 + i, 9:25, :], ext[3, 2 + i, 7:23, :]),
            beside(3, centre, False),
        ]
        sides = [(0.5 * (centre + a), 0.5 * (centre + b)) for a, b in sides]
        speed = [ext[c, 2 + i, 8:24, :] for c in range(3)]
        for c in range(3):
            here = speed[c]
            near = [
                [ext[c, 2 + i + m, 8:24, :] for m in (1, -1, 2, -2)],
                [ext[c, 2 + i, 8 + m : 24 + m, :] for m in (1, -1, 2, -2)],
                beside(c, here, True),
            ]
            change = None
            for axis in range(3):
                a1, b1, a2, b2 = near[axis]
                slope = (8.0 * (a1 - b1) - (a2 - b2)) * (1.0 / 12.0)
                term = sides[axis][0] * (a1 - here) - sides[axis][1] * (here - b1)
                term = term - speed[axis] * slope
                change = term if change is None else change + term
            u_next[c, i] = here + 0.2 * change
        return carry

    lax.fori_loop(0, 16, row, 0)

    for part in f_across:
        part.wait_recv()
    mine = f_plane[0]
    for s in range(1, 16):
        mine = mine + f_plane[s]
    f_mid[...] = mine
    f_deep[depth] = mine
    f_planes = [send(f_mid, f_deep.at[depth], device) for device in deeper]

    for part in deep:
        part.wait_recv()
    mine = deep_in[0]
    for d in range(1, 8):
        mine = mine + deep_in[d]
    own = pl.ds(pl.multiple_of(spot * 32, 32), 32)
    total[core, own, :] = mine
    gather = [
        send(total.at[core, own], total.at[core, own], plane(dy, dx)[1]) for dy, dx in steps
    ]

    for part in f_planes:
        part.wait_recv()
    mine = f_deep[0]
    for d in range(1, 8):
        mine = mine + f_deep[d]
    f_total[own32, :] = mine
    f_last = send(f_total.at[own32], f_total.at[own32], other)

    across = []
    for dy in range(4):
        for part, (sy, _) in zip(gather, steps):
            if sy == dy:
                part.wait_recv()
        rows = pl.ds(pl.multiple_of(((y + 4 - dy) % 4) * 128, 128), 128)
        across.append(send(total.at[core, rows], total.at[core, rows], other))
    f_last.wait_recv()
    grad_first[...] = f_total[:, :81]
    for part in across:
        part.wait_recv()

    for t in range(14):
        wide = 64 if t == 13 else 128
        grad_hidden[:, t * 128 : t * 128 + wide] = total[t // 7, (t % 7) * 64 : (t % 7) * 64 + 64, :wide]
    grad_last[...] = total[1, 448:449, :64]
    losses = total[0, 448:464, :]
    at = lax.broadcasted_iota(jnp.int32, (16, 128), 0)
    losses = jnp.where(at == (gy * 2 + role) * 2 + gx // 16, losses, 0.0)
    losses = jnp.sum(losses, axis=0, keepdims=True)
    losses = pltpu.roll(losses, (128 - (gx % 16) * 8) % 128, 1)
    slot_loss[0] = losses[:, :8]
    for part in started:
        part.wait_send()


SENDS = 7 + 1 + 15 + 1 + 15 + 7 + 7 + 15 + 1 + 4


def out_shapes():
    return (
        jax.ShapeDtypeStruct((3, 16, 16, 128), F32),
        jax.ShapeDtypeStruct((1, 1, 8), F32),
        jax.ShapeDtypeStruct((64, 81), F32),
        jax.ShapeDtypeStruct((64, 1728), F32),
        jax.ShapeDtypeStruct((1, 64), F32),
    )


def hand_out(*refs):
    moves = [pltpu.make_async_copy(refs[n], refs[5 + n], refs[10].at[n]) for n in range(5)]
    for move in moves:
        move.start()
    for move in moves:
        move.wait()


def on_device(velocity, target_visc, w_first, w_hidden, w_last, sample_owner, sample_block):
    vmem = pl.BlockSpec(memory_space=pltpu.VMEM)
    far = pl.BlockSpec(memory_space=pltpu.HBM)
    spread = spread_matrix()
    rows = (pool_matrix(), target_matrix(), spread[:, :256], spread[:, 256:], spread[:8, :256])
    consts = [jnp.asarray(np.concatenate(rows, 0)), jnp.asarray(first_selector())]
    args = [
        velocity, target_visc, w_first, w_hidden, w_last.reshape(1, 64),
        sample_owner.reshape(1, 256), sample_block.reshape(1, 256), *consts,
    ]
    outs = pl.pallas_call(
        whole_kernel,
        out_shape=out_shapes(),
        in_specs=[far] * 9,
        out_specs=(vmem,) * 5,
        scratch_shapes=[pltpu.VMEM(a.shape, a.dtype) for a in args] + [
            pltpu.VMEM((512, 128), F32),
            pltpu.VMEM((10, 64, 128), BF16),
            pltpu.VMEM((3, 512, 128), BF16),
            pltpu.VMEM((3, 256, 1152), BF16),
            pltpu.VMEM((3, 1152, 256), BF16),
            pltpu.VMEM((2, 10, 64, 1152), BF16),
            pltpu.VMEM((2, 10, 64, 1152), BF16),
            pltpu.VMEM((512, 512), F32),
            pltpu.VMEM((2, 512, 128), F32),
            pltpu.VMEM((2, 512, 128), F32),
            pltpu.VMEM((64, 128), F32),
            pltpu.VMEM((4, 20, 32, 128), F32),
            pltpu.VMEM((2, 7, 16, 128), F32),
            pltpu.VMEM((2, 7, 16, 128), F32),
            pltpu.VMEM((3, 16, 128), F32),
            pltpu.VMEM((3, 16, 128), F32),
            pltpu.VMEM((512, 128), F32),
            pltpu.VMEM((512, 128), F32),
            pltpu.VMEM((15, 32, 128), F32),
            pltpu.VMEM((32, 128), F32),
            pltpu.VMEM((8, 32, 128), F32),
            pltpu.VMEM((2, 512, 128), F32),
            pltpu.VMEM((32, 128), F32),
            pltpu.VMEM((32, 128), F32),
            pltpu.VMEM((16, 32, 128), F32),
            pltpu.VMEM((32, 128), F32),
            pltpu.VMEM((8, 32, 128), F32),
            pltpu.VMEM((64, 128), F32),
            pltpu.SemaphoreType.DMA((9,)),
            pltpu.SemaphoreType.DMA((2, SENDS)),
        ],
        compiler_params=pltpu.CompilerParams(
            vmem_limit_bytes=48 * 1024 * 1024, collective_id=0, has_side_effects=True
        ),
        name="whole",
    )(*args)
    outs = pl.pallas_call(
        hand_out,
        out_shape=out_shapes(),
        in_specs=[vmem] * 5,
        out_specs=(far,) * 5,
        scratch_shapes=[pltpu.SemaphoreType.DMA((5,))],
        compiler_params=pltpu.CompilerParams(vmem_limit_bytes=8 * 1024 * 1024),
        name="hand_out",
    )(*outs)
    u_next, slot_loss, grad_first, grad_hidden, grad_last = outs
    return (u_next, slot_loss, grad_first, grad_hidden, grad_last.reshape(64))


def solution(mesh):
    return jax.shard_map(
        on_device,
        mesh=mesh,
        in_specs=(
            P(None, "gx", "gy", "role"),
            P("gx", "gy", "role"),
            P(),
            P(),
            P(),
            P("gy", "role", None, None),
            P("gy", "role", None, None),
        ),
        out_specs=(P(None, "gx", "gy", "role"), P("gy", "role", "gx"), P(), P(), P()),
        check_vma=False,
    )
```

time: 60.5 us -> 52.8 us (0.87)
  local copies, waits for them, and re-layouts: 10.8 us -> 6.07 us
  Pallas kernels: 48.5 us -> 45.7 us
    unnamed x27 -> x18, local copies, waits for them, and re-layouts: 10.8 us -> 6.07 us
    pallas_call x2, Pallas kernels: 48.5 us -> 45.7 us  [the longest x1 44.8 us: on_device(): pl.pallas_call(whole_kernel, out_shape=out_shapes(), in_specs=[far] * 9,...]
where the time goes in v2:
time: 52.8 us; the launch traced here: 52.5 us
  Pallas kernels  45.7 us (87%)
  local copies, waits for them, and re-layouts  6.07 us (11%)
  between operations  0.67 us (1%)
    pallas_call x1, Pallas kernels, on_device(): pl.pallas_call(whole_kernel, out_shape=out_shapes(), in_specs=[far] * 9,...  44.8 us
    unnamed x18, local copies, waits for them, and re-layouts  6.07 us

profile of v2, /device:TPU:1, one launch (start us, length us, event | category | flops | bytes accessed | tf_op | source)
XLA Modules:
  0.0 52.5 jit_solution(14890533261116818068)
XLA Ops:
  0.6 0.0 copy-start.7
  0.6 0.0 copy-start.6
  0.7 0.0 copy-start.8
  0.7 0.7 %copy-done.7 = s32[1,1,256,1]{2,3,1,0:T(1,128)S(1)} copy-done((s32[1,1,256,1]{2,3,1,0:T(1,128)S(1)}, s32[1,1,256,1]{2,3,1,0:T(1,128)}, u32[]{:S(2)}) %copy-start.7) | copy-done | bytes 1048
  1.3 0.0 copy-done.6
  1.3 0.0 copy-done.8
  1.3 0.0 copy-start
  1.3 1.0 %copy-done = bf16[81,3072]{1,0:T(8,128)(2,1)S(1)} copy-done((bf16[81,3072]{1,0:T(8,128)(2,1)S(1)}, bf16[81,3072]{1,0:T(8,128)(2,1)}, u32[]{:S(2)}) %copy-start) | copy-done | bytes 497688
  2.4 0.0 copy-start.1
  2.4 1.0 %copy-done.1 = f32[3,16,16,128]{3,2,1,0:T(8,128)S(1)} copy-done((f32[3,16,16,128]{3,2,1,0:T(8,128)S(1)}, f32[3,16,16,128]{3,2,1,0:T(8,128)}, u32[]{:S(2)}) %copy-start.1) | copy-done | bytes 393240
  3.4 0.0 copy-start.2
  3.4 1.0 %copy-done.2 = bf16[712,256]{1,0:T(8,128)(2,1)S(1)} copy-done((bf16[712,256]{1,0:T(8,128)(2,1)S(1)}, bf16[712,256]{1,0:T(8,128)(2,1)}, u32[]{:S(2)}) %copy-start.2) | copy-done | bytes 364568
  4.4 0.0 copy-start.3
  4.4 0.9 %copy-done.3 = bf16[64,1728]{1,0:T(8,128)(2,1)S(1)} copy-done((bf16[64,1728]{1,0:T(8,128)(2,1)S(1)}, bf16[64,1728]{1,0:T(8,128)(2,1)}, u32[]{:S(2)}) %copy-start.3) | copy-done | bytes 221208
  5.3 0.0 copy-start.4
  5.3 0.7 %copy-done.4 = bf16[8,8,64]{2,1,0:T(8,128)(2,1)S(1)} copy-done((bf16[8,8,64]{2,1,0:T(8,128)(2,1)S(1)}, bf16[8,8,64]{2,1,0:T(8,128)(2,1)}, u32[]{:S(2)}) %copy-start.4) | copy-done | bytes 8216
  6.0 0.0 copy-start.5
  6.0 0.7 %copy-done.5 = bf16[64,81]{1,0:T(8,128)(2,1)S(1)} copy-done((bf16[64,81]{1,0:T(8,128)(2,1)S(1)}, bf16[64,81]{1,0:T(8,128)(2,1)}, u32[]{:S(2)}) %copy-start.5) | copy-done | bytes 10392
  6.7 44.8 %whole.1 = (f32[3,16,16,128]{3,2,1,0:T(8,128)S(1)}, f32[1,1,8]{2,1,0:T(1,128)S(1)}, f32[64,81]{1,0:T(8,128)S(1)}, f32[64,1728]{1,0:T(8,128)S(1)}, f32[1,64]{1,0:T(1,128)S(1)}) custom-call(f32[3,16,16,128]{3,2,1,0:T(8,128)S(1)} %copy-done.1, bf16[8,8,64]{2,1,0:T(8,128)(2,1)S(1)} %copy-done.4, bf16[64,81]{1,0:T(8,128)(2,1)S(1)} %copy-done.5, ...), custom_call_target="tpu_custom_call" | custom-call | tf_op jit(solution)/shard_map/whole/pallas_call | solution.py:559
  51.5 1.0 %hand_out.1 = (f32[3,16,16,128]{3,2,1,0:T(8,128)}, f32[1,1,8]{2,1,0:T(1,128)}, f32[64,81]{1,0:T(8,128)}, f32[64,1728]{1,0:T(8,128)}, f32[1,64]{1,0:T(1,128)}) custom-call(f32[3,16,16,128]{3,2,1,0:T(8,128)S(1)} %get-tuple-element.15.refs_0_, f32[1,1,8]{2,1,0:T(1,128)S(1)} %get-tuple-element.16.refs_1_, f32[64,81]{1,0:T(8,128)S(1)} %get-tuple-element.17.refs_2_, ...), custom_call_target="tpu_custom_call" | custom-call | tf_op jit(solution)/shard_map/hand_out/pallas_call | solution.py:601
Async XLA Ops:
  0.6 0.7 %copy-start.7 = (s32[1,1,256,1]{2,3,1,0:T(1,128)S(1)}, s32[1,1,256,1]{2,3,1,0:T(1,128)}, u32[]{:S(2)}) copy-start(s32[1,1,256,1]{2,3,1,0:T(1,128)} %param.15) | copy-start | bytes 3076
  0.6 0.7 %copy-start.6 = (s32[1,1,256,1]{2,3,1,0:T(1,128)S(1)}, s32[1,1,256,1]{2,3,1,0:T(1,128)}, u32[]{:S(2)}) copy-start(s32[1,1,256,1]{2,3,1,0:T(1,128)} %param.14) | copy-start | bytes 3076
  0.7 0.7 %copy-start.8 = (bf16[64]{0:T(256)(128)(2,1)S(1)}, bf16[64]{0:T(256)(128)(2,1)}, u32[]{:S(2)}) copy-start(bf16[64]{0:T(256)(128)(2,1)} %param.13) | copy-start | bytes 388
  1.3 1.0 %copy-start = (bf16[81,3072]{1,0:T(8,128)(2,1)S(1)}, bf16[81,3072]{1,0:T(8,128)(2,1)}, u32[]{:S(2)}) copy-start(bf16[81,3072]{1,0:T(8,128)(2,1)} %constant.5.clone.refs_8_) | copy-start | bytes 1492996
  2.4 1.0 %copy-start.1 = (f32[3,16,16,128]{3,2,1,0:T(8,128)S(1)}, f32[3,16,16,128]{3,2,1,0:T(8,128)}, u32[]{:S(2)}) copy-start(f32[3,16,16,128]{3,2,1,0:T(8,128)} %refs_0_.1) | copy-start | bytes 1179652
  3.4 1.0 %copy-start.2 = (bf16[712,256]{1,0:T(8,128)(2,1)S(1)}, bf16[712,256]{1,0:T(8,128)(2,1)}, u32[]{:S(2)}) copy-start(bf16[712,256]{1,0:T(8,128)(2,1)} %constant.4.clone.refs_7_) | copy-start | bytes 1093636
  4.4 0.9 %copy-start.3 = (bf16[64,1728]{1,0:T(8,128)(2,1)S(1)}, bf16[64,1728]{1,0:T(8,128)(2,1)}, u32[]{:S(2)}) copy-start(bf16[64,1728]{1,0:T(8,128)(2,1)} %refs_3_.1) | copy-start | bytes 663556
  5.3 0.7 %copy-start.4 = (bf16[8,8,64]{2,1,0:T(8,128)(2,1)S(1)}, bf16[8,8,64]{2,1,0:T(8,128)(2,1)}, u32[]{:S(2)}) copy-start(bf16[8,8,64]{2,1,0:T(8,128)(2,1)} %refs_1_.1) | copy-start | bytes 24580
  6.0 0.7 %copy-start.5 = (bf16[64,81]{1,0:T(8,128)(2,1)S(1)}, bf16[64,81]{1,0:T(8,128)(2,1)}, u32[]{:S(2)}) copy-start(bf16[64,81]{1,0:T(8,128)(2,1)} %refs_2_.1) | copy-start | bytes 31108

commit v3 on v2

--- a/solution.py
+++ b/solution.py
@@ -82,6 +82,21 @@
         whole = whole.reshape(8, 64, 384)
         for j in range(3):
             store[half, 1:9, :, j * 384 : (j + 1) * 384] = shift_y(whole, j - 1).astype(BF16)
+
+
+def widen_pairs(store, field):
+    low = lane_of((512, 128)) < 64
+    zero = jnp.zeros((64, 768), BF16)
+    none = jnp.zeros((512, 128), F32)
+    pairs = [field[:, p * 128 : (p + 1) * 128] for p in range(4)]
+    turned = [none] + [pltpu.roll(p, 64, 1) for p in pairs] + [none]
+    for p in range(4):
+        store[p, 0] = zero
+        store[p, 9] = zero
+        near = jnp.where(low, turned[p], turned[p + 2])
+        whole = jnp.concatenate([pairs[p], near], axis=1).reshape(8, 64, 256)
+        for j in range(3):
+            store[p, 1:9, :, j * 256 : (j + 1) * 256] = shift_y(whole, j - 1).astype(BF16)
 
 
 def rows_of(store, half, i):
@@ -130,11 +145,13 @@
 
 def whole_kernel(*refs):
     sources, refs = refs[:9], refs[9:]
-    (u_next, slot_loss, grad_first, grad_hidden, grad_last), refs = refs[:5], refs[5:]
+    results, refs = refs[:5], refs[5:]
     held_in, refs = refs[:9], refs[9:]
     vel, target, w_first, w_hidden, w_last, owner, block, fixed, sel = held_in
+    held_out, refs = refs[:5], refs[5:]
+    u_next, slot_loss, grad_first, grad_hidden, grad_last = held_out
     (
-        filt, first_in, w_one, ahead, back, wide_act, wide_del, slope_one, eddy_z,
+        filt, first_in, w_one, ahead, back, wide_act, wide_del, slope_one, pair_act, eddy_z,
         sums, first_sums, ext, y_out, y_in, z_out, z_in,
         half_in, half_sum, chunk_in, chunk_sum, deep_in, total,
         f_in, f_sum, f_plane, f_mid, f_deep, f_total,
@@ -148,6 +165,11 @@
     for n in (3, 0, 2, 8, 7, 1, 4, 5, 6):
         loads[n].start()
 
+    def hand_over(n):
+        move = pltpu.make_async_copy(held_out[n], results[n], local_sems.at[9 + n])
+        move.start()
+        return move
+
     gx, gy, role = lax.axis_index("gx"), lax.axis_index("gy"), lax.axis_index("role")
     depth, y = gx // 4, gx % 4
     x, core = (gy // 2) * 2 + role, gy % 2
@@ -157,8 +179,10 @@
         to_y, to_x = (y + dy) % 4, (x + dx) % 4
         return to_y * 4 + to_x, (depth * 4 + to_y, (to_x // 2) * 2 + core, to_x % 2)
 
+    reach = (0, 1, 2, 1)
     steps = [(dy, dx) for dy in range(4) for dx in range(4) if dy or dx]
-    deeper = [(((depth + d) % 8) * 4 + y, gy, role) for d in range(1, 8)]
+    steps.sort(key=lambda s: -reach[s[0]] - reach[s[1]])
+    deeper = [(((depth + d) % 8) * 4 + y, gy, role) for d in (4, 3, 5, 2, 6, 1, 7)]
     other = (gx, gy - core + 1 - core, role)
     x_up, x_down = ((gx + 1) % 32, gy, role), ((gx + 31) % 32, gy, role)
     y_up, y_down = (gx, (gy + 1) % 4, role), (gx, (gy + 3) % 4, role)
@@ -236,7 +260,9 @@
         pre = term if pre is None else pre + term
     sig = 1.0 / (1.0 + jnp.exp(-pre))
     slope_one[...] = sig * (1.0 + pre * (1.0 - sig))
-    widen(wide_act, (pre * sig).astype(BF16).astype(F32))
+    acts = (pre * sig).astype(BF16).astype(F32)
+    widen(wide_act, acts)
+    widen_pairs(pair_act, acts)
 
     slot_of, base_of = (0, 0, 1, 2), (0, 16, 0, 0)
     lane16 = lane_of((16, 128))
@@ -295,8 +321,11 @@
         delta = (wl * d_logit * slope).astype(BF16).astype(F32)
         deltas.append(delta)
         scaled = (delta.reshape(64, 8, 256) * times.reshape(1, 8, 1)).reshape(512, 256)
-        low = scaled - scaled.astype(BF16).astype(F32)
-        parts.append(jnp.concatenate([scaled.T.astype(BF16), low.T.astype(BF16)], axis=0))
+        high = scaled.astype(BF16)
+        low = (scaled - high.astype(F32)).astype(BF16)
+        for p in range(2):
+            cut = slice(p * 128, p * 128 + 128)
+            parts.append(jnp.concatenate([high[:, cut].T, low[:, cut].T], axis=0))
     widen(wide_del, jnp.concatenate(deltas, axis=1))
 
     lane = lane_of((64, 128))
@@ -340,22 +369,19 @@
     held_a = None
     for i in range(3):
         grad = None
-        for half in range(2):
-            term = dot(parts[half], rows_of(wide_act, half, i))
+        for p in range(4):
+            term = dot(parts[p], pair_act[p, i : i + 8].reshape(512, 768))
             grad = term if grad is None else grad + term
-        grad = grad[:256] + grad[256:]
+        grad = grad[:128] + grad[128:]
         for j in range(3):
             k = 3 * i + j
             g = [
-                [grad[zo * 64 : zo * 64 + 64, j * 384 + p * 128 : j * 384 + p * 128 + 128] for p in range(3)]
-                for zo in range(4)
+                [grad[zo * 64 : zo * 64 + 64, j * 256 + p * 128 : j * 256 + p * 128 + 128] for p in range(2)]
+                for zo in range(2)
             ]
-            bc = g[0][0] + g[2][1]
-            ab = g[1][0] + g[3][1]
-            cb = pltpu.roll(bc, 64, 1)
-            a_low = g[0][2] + pltpu.roll(g[2][0], 64, 1)
-            ab = ab + jnp.where(is_low, a_low, cb)
-            c_low = cb + g[1][1] + pltpu.roll(g[3][2], 64, 1)
+            cb = pltpu.roll(g[0][0], 64, 1)
+            ab = g[1][0] + jnp.where(is_low, g[0][1], cb)
+            c_low = cb + pltpu.roll(g[1][1], 64, 1)
             t = 3 * k // 2
             if k % 2 == 0:
                 column(t, ab)
@@ -376,8 +402,9 @@
             d_act = term if d_act is None else d_act + term
         d_first = (d_act * slope_one[:, half * 256 : half * 256 + 256]).astype(BF16).astype(F32)
         scaled = (d_first.reshape(64, 8, 256) * times.reshape(1, 8, 1)).reshape(512, 256)
-        low = scaled - scaled.astype(BF16).astype(F32)
-        firsts.append((scaled.T.astype(BF16), low.T.astype(BF16)))
+        high = scaled.astype(BF16)
+        low = (scaled - high.astype(F32)).astype(BF16)
+        firsts.append((high.T, low.T))
         if half == 0:
             first.wait_recv()
             half_sum[...] = sums[core] + half_in[...]
@@ -470,6 +497,7 @@
         return carry
 
     lax.fori_loop(0, 16, row, 0)
+    moves = [hand_over(0)]
 
     for part in f_across:
         part.wait_recv()
@@ -508,6 +536,7 @@
         across.append(send(total.at[core, rows], total.at[core, rows], other))
     f_last.wait_recv()
     grad_first[...] = f_total[:, :81]
+    moves.append(hand_over(2))
     for part in across:
         part.wait_recv()
 
@@ -521,8 +550,11 @@
     losses = jnp.sum(losses, axis=0, keepdims=True)
     losses = pltpu.roll(losses, (128 - (gx % 16) * 8) % 128, 1)
     slot_loss[0] = losses[:, :8]
+    moves += [hand_over(n) for n in (3, 4, 1)]
     for part in started:
         part.wait_send()
+    for move in moves:
+        move.wait()
 
 
 SENDS = 7 + 1 + 15 + 1 + 15 + 7 + 7 + 15 + 1 + 4
@@ -539,16 +571,21 @@
 
 
 def hand_out(*refs):
-    moves = [pltpu.make_async_copy(refs[n], refs[5 + n], refs[10].at[n]) for n in range(5)]
-    for move in moves:
-        move.start()
-    for move in moves:
-        move.wait()
+    sources, results, held, sems = refs[:5], refs[5:10], refs[10:15], refs[15]
+    loads = [pltpu.make_async_copy(sources[n], held[n], sems.at[0, n]) for n in range(5)]
+    stores = [pltpu.make_async_copy(held[n], results[n], sems.at[1, n]) for n in range(5)]
+    order = (0, 3, 2, 1, 4)
+    for n in order:
+        loads[n].start()
+    for n in order:
+        loads[n].wait()
+        stores[n].start()
+    for n in order:
+        stores[n].wait()
 
 
 def on_device(velocity, target_visc, w_first, w_hidden, w_last, sample_owner, sample_block):
-    vmem = pl.BlockSpec(memory_space=pltpu.VMEM)
-    far = pl.BlockSpec(memory_space=pltpu.HBM)
+    anywhere = pl.BlockSpec(memory_space=pl.ANY)
     spread = spread_matrix()
     rows = (pool_matrix(), target_matrix(), spread[:, :256], spread[:, 256:], spread[:8, :256])
     consts = [jnp.asarray(np.concatenate(rows, 0)), jnp.asarray(first_selector())]
@@ -559,9 +596,9 @@
     outs = pl.pallas_call(
         whole_kernel,
         out_shape=out_shapes(),
-        in_specs=[far] * 9,
-        out_specs=(vmem,) * 5,
-        scratch_shapes=[pltpu.VMEM(a.shape, a.dtype) for a in args] + [
+        in_specs=[anywhere] * 9,
+        out_specs=(anywhere,) * 5,
+        scratch_shapes=[pltpu.VMEM(a.shape, a.dtype) for a in args + list(out_shapes())] + [
             pltpu.VMEM((512, 128), F32),
             pltpu.VMEM((10, 64, 128), BF16),
             pltpu.VMEM((3, 512, 128), BF16),
@@ -570,6 +607,7 @@
             pltpu.VMEM((2, 10, 64, 1152), BF16),
             pltpu.VMEM((2, 10, 64, 1152), BF16),
             pltpu.VMEM((512, 512), F32),
+            pltpu.VMEM((4, 10, 64, 768), BF16),
             pltpu.VMEM((2, 512, 128), F32),
             pltpu.VMEM((2, 512, 128), F32),
             pltpu.VMEM((64, 128), F32),
@@ -590,21 +628,22 @@
             pltpu.VMEM((32, 128), F32),
             pltpu.VMEM((8, 32, 128), F32),
             pltpu.VMEM((64, 128), F32),
-            pltpu.SemaphoreType.DMA((9,)),
+            pltpu.SemaphoreType.DMA((14,)),
             pltpu.SemaphoreType.DMA((2, SENDS)),
         ],
         compiler_params=pltpu.CompilerParams(
-            vmem_limit_bytes=48 * 1024 * 1024, collective_id=0, has_side_effects=True
+            vmem_limit_bytes=60 * 1024 * 1024, collective_id=0, has_side_effects=True
         ),
         name="whole",
     )(*args)
     outs = pl.pallas_call(
         hand_out,
         out_shape=out_shapes(),
-        in_specs=[vmem] * 5,
-        out_specs=(far,) * 5,
-        scratch_shapes=[pltpu.SemaphoreType.DMA((5,))],
-        compiler_params=pltpu.CompilerParams(vmem_limit_bytes=8 * 1024 * 1024),
+        in_specs=[anywhere] * 5,
+        out_specs=(anywhere,) * 5,
+        scratch_shapes=[pltpu.VMEM(a.shape, a.dtype) for a in out_shapes()]
+        + [pltpu.SemaphoreType.DMA((2, 5))],
+        compiler_params=pltpu.CompilerParams(vmem_limit_bytes=60 * 1024 * 1024),
         name="hand_out",
     )(*outs)
     u_next, slot_loss, grad_first, grad_hidden, grad_last = outs

time: 52.8 us -> 44.7 us (0.85)
  local copies, waits for them, and re-layouts: 6.07 us -> 0 us
  Pallas kernels: 45.7 us -> 43.9 us
    unnamed x18 -> x0, local copies, waits for them, and re-layouts: 6.07 us -> none
    pallas_call x2, Pallas kernels: 45.7 us -> 43.9 us  [the longest x1 41.9 us: on_device(): pl.pallas_call(whole_kernel, out_shape=out_shapes(), in_specs=[anywhere]...]
where the time goes in v3:
time: 44.7 us; the launch traced here: 44.6 us
  Pallas kernels  43.9 us (98%)
  between operations  0.64 us (1%)
    pallas_call x1, Pallas kernels, on_device(): pl.pallas_call(whole_kernel, out_shape=out_shapes(), in_specs=[anywhere]...  41.9 us
    pallas_call x1, Pallas kernels, on_device(): pl.pallas_call(hand_out, out_shape=out_shapes(), in_specs=[anywhere] * 5,...  2 us

profile of v3, /device:TPU:1, one launch (start us, length us, event | category | flops | bytes accessed | tf_op | source)
XLA Modules:
  0.0 44.6 jit_solution(7555106353523638991)
XLA Ops:
  0.6 41.9 %whole.1 = (f32[3,16,16,128]{3,2,1,0:T(8,128)}, f32[1,1,8]{2,1,0:T(1,128)}, f32[64,81]{1,0:T(8,128)}, f32[64,1728]{1,0:T(8,128)}, f32[1,64]{1,0:T(1,128)}) custom-call(f32[3,16,16,128]{3,2,1,0:T(8,128)} %refs_0_.1, bf16[8,8,64]{2,1,0:T(8,128)(2,1)} %refs_1_.1, bf16[64,81]{1,0:T(8,128)(2,1)} %refs_2_.1, bf16[64,1728]{1,0:T(8,128)(2,1)} %refs_3_.1, ...), custom_call_target="tpu_custom_call" | custom-call | tf_op jit(solution)/shard_map/whole/pallas_call | solution.py:596
  42.6 2.0 %hand_out.1 = (f32[3,16,16,128]{3,2,1,0:T(8,128)}, f32[1,1,8]{2,1,0:T(1,128)}, f32[64,81]{1,0:T(8,128)}, f32[64,1728]{1,0:T(8,128)}, f32[1,64]{1,0:T(1,128)}) custom-call(f32[3,16,16,128]{3,2,1,0:T(8,128)} %get-tuple-element.15.refs_0_, f32[1,1,8]{2,1,0:T(1,128)} %get-tuple-element.16.refs_1_, f32[64,81]{1,0:T(8,128)} %get-tuple-element.17.refs_2_, ...), custom_call_target="tpu_custom_call" | custom-call | tf_op jit(solution)/shard_map/hand_out/pallas_call | solution.py:639

commit v4 on v3

--- a/solution.py
+++ b/solution.py
@@ -39,8 +39,8 @@
 
 def spread_matrix():
     row = np.arange(128)[:, None]
-    lane = np.arange(512)[None, :]
-    return (row == 24 + lane // 64).astype(jnp.bfloat16)
+    lane = np.arange(256)[None, :]
+    return (row == 24 + lane // 128 * 4 + lane // 2 % 4).astype(jnp.bfloat16)
 
 
 def first_selector():
@@ -69,19 +69,21 @@
 
 
 def widen(store, field):
-    lane = lane_of((512, 128))
-    zero = jnp.zeros((64, 1152), BF16)
-    near = [
-        jnp.where(lane >= 64, pltpu.roll(field[:, 256:384], 64, 1), 0.0),
-        jnp.where(lane < 64, pltpu.roll(field[:, 128:256], 64, 1), 0.0),
-    ]
+    low = lane_of((8, 64, 128)) < 64
+    zero = jnp.zeros((64, 960), BF16)
     for half in range(2):
         store[half, 0] = zero
         store[half, 9] = zero
-        whole = jnp.concatenate([field[:, half * 256 : half * 256 + 256], near[half]], axis=1)
-        whole = whole.reshape(8, 64, 384)
+        main = field[:, half * 256 : half * 256 + 256].reshape(8, 64, 256)
+        next_z = field[:, 256:384] if half == 0 else field[:, 128:256]
+        turned = pltpu.roll(next_z, 64, 1).reshape(8, 64, 128)
+        next_z = next_z.reshape(8, 64, 128)
+        in_low, in_high = (next_z, turned) if half == 0 else (turned, next_z)
         for j in range(3):
-            store[half, 1:9, :, j * 384 : (j + 1) * 384] = shift_y(whole, j - 1).astype(BF16)
+            store[half, 1:9, :, j * 256 : (j + 1) * 256] = shift_y(main, j - 1).astype(BF16)
+        edge = jnp.where(low, shift_y(in_low, -1), in_high)
+        store[half, 1:9, :, 768:896] = edge.astype(BF16)
+        store[half, 1:9, :, 896:960] = shift_y(in_low, 1)[:, :, :64].astype(BF16)
 
 
 def widen_pairs(store, field):
@@ -100,7 +102,7 @@
 
 
 def rows_of(store, half, i):
-    return store[half, i : i + 8].reshape(512, 1152)
+    return store[half, i : i + 8].reshape(512, 960)
 
 
 def place_weights(w_hidden, ahead, back):
@@ -112,6 +114,7 @@
     tiles.append(jnp.concatenate([last, last], axis=1))
     tiles = [t.astype(F32) for t in tiles]
     swapped = [pltpu.roll(t, 64, 1) for t in tiles]
+    lows, highs = [], []
     for j in range(9):
         t = 3 * j // 2
         if j % 2 == 0:
@@ -124,33 +127,46 @@
             ab = jnp.where(low, swapped[t], swapped[t + 1])
             c_low, c_high = swapped[t + 1], tiles[t + 1]
             a_low, a_high = swapped[t], tiles[t]
+        lows.append((c_low, a_low))
+        highs.append((c_high, a_high))
         c_0 = jnp.where(low, c_low, 0.0).astype(BF16)
-        o_c = jnp.where(low, 0.0, c_high).astype(BF16)
-        a_0 = jnp.where(low, a_low, 0.0).astype(BF16)
         o_a = jnp.where(low, 0.0, a_high).astype(BF16)
         ab = ab.astype(BF16)
         bc = bc.astype(BF16)
-        rows = [(bc, zero, a_0), (ab, c_0, zero), (o_a, bc, zero), (zero, ab, o_c)]
-        for zo in range(4):
-            for part in range(3):
-                start = (j % 3) * 384 + part * 128
-                ahead[j // 3, zo * 64 : (zo + 1) * 64, start : start + 128] = rows[zo][part]
+        rows = [(bc, zero), (ab, c_0), (o_a, bc), (zero, ab)]
         flip = 8 - j
-        rows = [(bc, zero), (ab, c_0), (o_a, bc), (zero, ab), (c_0, zero), (zero, o_a)]
-        for zi in range(6):
-            start = (flip % 3) * 384 + zi * 64
-            for part in range(2):
-                back[flip // 3, start : start + 64, part * 128 : (part + 1) * 128] = rows[zi][part]
+        for half in range(2):
+            for z in range(4):
+                at = slice(z * 64, (z + 1) * 64)
+                for part in range(2):
+                    start = (j % 3) * 256 + part * 128
+                    ahead[half, j // 3, at, start : start + 128] = rows[z][part]
+                    start = (flip % 3) * 256 + z * 64
+                    cut = slice(part * 128, (part + 1) * 128)
+                    back[half, flip // 3, start : start + 64, cut] = rows[z][part]
+        start = 768 + (flip % 3) * 64
+        back[0, flip // 3, start : start + 64, 0:128] = zero
+        back[0, flip // 3, start : start + 64, 128:256] = o_a
+        back[1, flip // 3, start : start + 64, 0:128] = c_0
+        back[1, flip // 3, start : start + 64, 128:256] = zero
+    for half in range(2):
+        for i in range(3):
+            edge = jnp.where(low, lows[3 * i][half], highs[3 * i + 1][half]).astype(BF16)
+            end = lows[3 * i + 2][half][:, :64].astype(BF16)
+            for z in range(4):
+                at = slice(z * 64, (z + 1) * 64)
+                here = z == (3 if half == 0 else 0)
+                ahead[half, i, at, 768:896] = edge if here else zero
+                ahead[half, i, at, 896:960] = end if here else zero[:, :64]
 
 
 def whole_kernel(*refs):
     sources, refs = refs[:9], refs[9:]
-    results, refs = refs[:5], refs[5:]
+    (u_result, f_result, result), refs = refs[:3], refs[3:]
     held_in, refs = refs[:9], refs[9:]
     vel, target, w_first, w_hidden, w_last, owner, block, fixed, sel = held_in
-    held_out, refs = refs[:5], refs[5:]
-    u_next, slot_loss, grad_first, grad_hidden, grad_last = held_out
     (
+        u_next,
         filt, first_in, w_one, ahead, back, wide_act, wide_del, slope_one, pair_act, eddy_z,
         sums, first_sums, ext, y_out, y_in, z_out, z_in,
         half_in, half_sum, chunk_in, chunk_sum, deep_in, total,
@@ -165,10 +181,11 @@
     for n in (3, 0, 2, 8, 7, 1, 4, 5, 6):
         loads[n].start()
 
-    def hand_over(n):
-        move = pltpu.make_async_copy(held_out[n], results[n], local_sems.at[9 + n])
-        move.start()
-        return move
+    moves = []
+
+    def hand_over(src, dst):
+        moves.append(pltpu.make_async_copy(src, dst, local_sems.at[9 + len(moves)]))
+        moves[-1].start()
 
     gx, gy, role = lax.axis_index("gx"), lax.axis_index("gy"), lax.axis_index("role")
     depth, y = gx // 4, gx % 4
@@ -205,18 +222,15 @@
         part.start()
         return part
 
-    loads[3].wait()
+    for n in (3, 0, 2, 8, 7, 1, 4, 5, 6):
+        loads[n].wait()
     place_weights(w_hidden, ahead, back)
-    loads[2].wait()
-    loads[8].wait()
     placed = dot(w_first[...], sel[...]).astype(BF16)
     for i in range(3):
         for zo in range(8):
             at = (i * 8 + zo) * 128
             w_one[i, zo * 64 : (zo + 1) * 64, :] = placed[:, at : at + 128]
 
-    for n in (0, 7, 1, 4, 5, 6):
-        loads[n].wait()
     pooled = []
     for comp in range(3):
         summed = None
@@ -243,8 +257,7 @@
             tile = pltpu.roll(tile, 128 - 32 * (b % 4), 1)
         filt[pl.ds(b, 64, stride=8), :] = tile
     held = filt[...]
-    held16 = held.astype(BF16)
-    targets = jnp.concatenate([dot(held16, fixed[448:576]), dot(held16, fixed[576:704])], axis=1)
+    targets = dot(held.astype(BF16), fixed[448:576])
     lane = lane_of((512, 128))
     inputs = jnp.where(lane < 24, held, 0.0).reshape(8, 64, 128)
     near = shift_y(inputs, -1)
@@ -286,37 +299,34 @@
 
     wl = w_last[...].astype(F32)
     wl = jnp.concatenate([wl, wl, wl, wl], axis=1)
-    rows_iota = lax.broadcasted_iota(jnp.int32, (384, 256), 0)
-    lanes_iota = lax.broadcasted_iota(jnp.int32, (384, 256), 1)
-    cell = jnp.where(rows_iota < 256, rows_iota // 64, (rows_iota // 2) % 4)
-    out_map = jnp.where(cell == lanes_iota // 64, wl, 0.0).astype(BF16)
+    rows_iota = lax.broadcasted_iota(jnp.int32, (128, 256), 0)
+    lanes_iota = lax.broadcasted_iota(jnp.int32, (128, 256), 1)
+    out_map = jnp.where(rows_iota // 2 % 4 == lanes_iota // 64, wl, 0.0).astype(BF16)
+    repeat = jnp.where(rows_iota == lanes_iota // 64 * 2, 1.0, 0.0).astype(BF16)
 
     number = lax.broadcasted_iota(jnp.int32, (8, 256), 0)
     drawn = jnp.where((owner[...] == gx) & (block[...] == number), 1.0, 0.0)
     times = jnp.sum(drawn, axis=1, keepdims=True)
 
-    loss = jnp.zeros((8, 256), F32)
+    loss = jnp.zeros((8, 128), F32)
     last = jnp.zeros((8, 256), F32)
     deltas, parts = [], []
     for half in range(2):
         pre = None
         for i in range(3):
-            term = dot(rows_of(wide_act, half, i), ahead[i], NT)
+            term = dot(rows_of(wide_act, half, i), ahead[half, i], NT)
             pre = term if pre is None else pre + term
         sig = 1.0 / (1.0 + jnp.exp(-pre))
         act = (pre * sig).astype(BF16)
         slope = sig * (1.0 + pre * (1.0 - sig))
-        both = dot(act, out_map, NT)
-        logits = both[:, :256]
-        eddy_z[half] = 0.5 * (
-            jnp.maximum(both[:, 256:], 0.0) + jnp.log1p(jnp.exp(-jnp.abs(both[:, 256:])))
-        )
+        logits = dot(act, out_map, NT)
         small = jnp.exp(-jnp.abs(logits))
         eddy = 0.5 * (jnp.maximum(logits, 0.0) + jnp.log1p(small))
+        eddy_z[half] = eddy
         gate = jnp.where(logits >= 0, 1.0, small) / (1.0 + small)
-        error = eddy - targets[:, half * 256 : half * 256 + 256]
-        loss = loss + jnp.sum((error * error).reshape(64, 8, 256), axis=0)
-        d_logit = (error * gate * (1.0 / (256 * 512))).astype(BF16).astype(F32)
+        error = eddy - targets[:, half * 128 : half * 128 + 128]
+        loss = loss + jnp.sum((error * error).reshape(64, 8, 128), axis=0)
+        d_logit = dot((error * gate * (1.0 / (256 * 512))).astype(BF16), repeat)
         last = last + jnp.sum((d_logit * act.astype(F32)).reshape(64, 8, 256), axis=0)
         delta = (wl * d_logit * slope).astype(BF16).astype(F32)
         deltas.append(delta)
@@ -351,7 +361,7 @@
         send(z_out, z_in, z_side),
     ]
 
-    per_block = jnp.sum(loss, axis=1, keepdims=True) * (1.0 / (64 * 512))
+    per_block = jnp.sum(loss, axis=1, keepdims=True) * (1.0 / (32 * 512))
     by_slot = jnp.sum(drawn * per_block, axis=0, keepdims=True)
     group = gy * 2 + role
     at = lax.broadcasted_iota(jnp.int32, (64, 128), 0)
@@ -398,7 +408,7 @@
     for half in range(2):
         d_act = None
         for i in range(3):
-            term = dot(rows_of(wide_del, half, i), back[i])
+            term = dot(rows_of(wide_del, half, i), back[half, i])
             d_act = term if d_act is None else d_act + term
         d_first = (d_act * slope_one[:, half * 256 : half * 256 + 256]).astype(BF16).astype(F32)
         scaled = (d_first.reshape(64, 8, 256) * times.reshape(1, 8, 1)).reshape(512, 256)
@@ -497,7 +507,7 @@
         return carry
 
     lax.fori_loop(0, 16, row, 0)
-    moves = [hand_over(0)]
+    hand_over(u_next, u_result)
 
     for part in f_across:
         part.wait_recv()
@@ -533,24 +543,12 @@
             if sy == dy:
                 part.wait_recv()
         rows = pl.ds(pl.multiple_of(((y + 4 - dy) % 4) * 128, 128), 128)
-        across.append(send(total.at[core, rows], total.at[core, rows], other))
+        across.append(send(total.at[core, rows], result.at[core, rows], other))
+    hand_over(total.at[core], result.at[core])
     f_last.wait_recv()
-    grad_first[...] = f_total[:, :81]
-    moves.append(hand_over(2))
+    hand_over(f_total, f_result)
     for part in across:
         part.wait_recv()
-
-    for t in range(14):
-        wide = 64 if t == 13 else 128
-        grad_hidden[:, t * 128 : t * 128 + wide] = total[t // 7, (t % 7) * 64 : (t % 7) * 64 + 64, :wide]
-    grad_last[...] = total[1, 448:449, :64]
-    losses = total[0, 448:464, :]
-    at = lax.broadcasted_iota(jnp.int32, (16, 128), 0)
-    losses = jnp.where(at == (gy * 2 + role) * 2 + gx // 16, losses, 0.0)
-    losses = jnp.sum(losses, axis=0, keepdims=True)
-    losses = pltpu.roll(losses, (128 - (gx % 16) * 8) % 128, 1)
-    slot_loss[0] = losses[:, :8]
-    moves += [hand_over(n) for n in (3, 4, 1)]
     for part in started:
         part.wait_send()
     for move in moves:
@@ -570,42 +568,74 @@
     )
 
 
-def hand_out(*refs):
-    sources, results, held, sems = refs[:5], refs[5:10], refs[10:15], refs[15]
-    loads = [pltpu.make_async_copy(sources[n], held[n], sems.at[0, n]) for n in range(5)]
-    stores = [pltpu.make_async_copy(held[n], results[n], sems.at[1, n]) for n in range(5)]
-    order = (0, 3, 2, 1, 4)
-    for n in order:
-        loads[n].start()
-    for n in order:
-        loads[n].wait()
-        stores[n].start()
-    for n in order:
-        stores[n].wait()
+def hand_out(
+    u_source, f_source, source, u_result, loss_result, first_result, hidden_result, last_result,
+    u_held, f_held, held, slot_loss, grad_first, grad_hidden, grad_last, sems,
+):
+    gx, gy, role = lax.axis_index("gx"), lax.axis_index("gy"), lax.axis_index("role")
+    loads = [
+        pltpu.make_async_copy(source, held, sems.at[0]),
+        pltpu.make_async_copy(u_source, u_held, sems.at[1]),
+        pltpu.make_async_copy(f_source, f_held, sems.at[2]),
+    ]
+    stores = [
+        pltpu.make_async_copy(grad_hidden, hidden_result, sems.at[3]),
+        pltpu.make_async_copy(u_held, u_result, sems.at[4]),
+        pltpu.make_async_copy(grad_first, first_result, sems.at[5]),
+        pltpu.make_async_copy(grad_last, last_result, sems.at[6]),
+        pltpu.make_async_copy(slot_loss, loss_result, sems.at[7]),
+    ]
+    for load in loads:
+        load.start()
+    loads[0].wait()
+    for t in range(14):
+        wide = 64 if t == 13 else 128
+        rows = slice((t % 7) * 64, (t % 7) * 64 + 64)
+        grad_hidden[:, t * 128 : t * 128 + wide] = held[t // 7, rows, :wide]
+    stores[0].start()
+    loads[1].wait()
+    stores[1].start()
+    loads[2].wait()
+    grad_first[...] = f_held[:, :81]
+    grad_last[...] = held[1, 448:449, :64]
+    losses = held[0, 448:464, :]
+    at = lax.broadcasted_iota(jnp.int32, (16, 128), 0)
+    losses = jnp.where(at == (gy * 2 + role) * 2 + gx // 16, losses, 0.0)
+    losses = jnp.sum(losses, axis=0, keepdims=True)
+    losses = pltpu.roll(losses, (128 - (gx % 16) * 8) % 128, 1)
+    slot_loss[0] = losses[:, :8]
+    for store in stores[2:]:
+        store.start()
+    for store in stores:
+        store.wait()
 
 
 def on_device(velocity, target_visc, w_first, w_hidden, w_last, sample_owner, sample_block):
     anywhere = pl.BlockSpec(memory_space=pl.ANY)
     spread = spread_matrix()
-    rows = (pool_matrix(), target_matrix(), spread[:, :256], spread[:, 256:], spread[:8, :256])
+    rows = (pool_matrix(), target_matrix(), spread, spread[:8])
     consts = [jnp.asarray(np.concatenate(rows, 0)), jnp.asarray(first_selector())]
     args = [
         velocity, target_visc, w_first, w_hidden, w_last.reshape(1, 64),
         sample_owner.reshape(1, 256), sample_block.reshape(1, 256), *consts,
     ]
+    sums = [
+        jax.ShapeDtypeStruct(shape, F32) for shape in ((3, 16, 16, 128), (64, 128), (2, 512, 128))
+    ]
     outs = pl.pallas_call(
         whole_kernel,
-        out_shape=out_shapes(),
+        out_shape=sums,
         in_specs=[anywhere] * 9,
-        out_specs=(anywhere,) * 5,
-        scratch_shapes=[pltpu.VMEM(a.shape, a.dtype) for a in args + list(out_shapes())] + [
+        out_specs=(anywhere,) * 3,
+        scratch_shapes=[pltpu.VMEM(a.shape, a.dtype) for a in args] + [
+            pltpu.VMEM((3, 16, 16, 128), F32),
             pltpu.VMEM((512, 128), F32),
             pltpu.VMEM((10, 64, 128), BF16),
             pltpu.VMEM((3, 512, 128), BF16),
-            pltpu.VMEM((3, 256, 1152), BF16),
-            pltpu.VMEM((3, 1152, 256), BF16),
-            pltpu.VMEM((2, 10, 64, 1152), BF16),
-            pltpu.VMEM((2, 10, 64, 1152), BF16),
+            pltpu.VMEM((2, 3, 256, 960), BF16),
+            pltpu.VMEM((2, 3, 960, 256), BF16),
+            pltpu.VMEM((2, 10, 64, 960), BF16),
+            pltpu.VMEM((2, 10, 64, 960), BF16),
             pltpu.VMEM((512, 512), F32),
             pltpu.VMEM((4, 10, 64, 768), BF16),
             pltpu.VMEM((2, 512, 128), F32),
@@ -628,7 +658,7 @@
             pltpu.VMEM((32, 128), F32),
             pltpu.VMEM((8, 32, 128), F32),
             pltpu.VMEM((64, 128), F32),
-            pltpu.SemaphoreType.DMA((14,)),
+            pltpu.SemaphoreType.DMA((12,)),
             pltpu.SemaphoreType.DMA((2, SENDS)),
         ],
         compiler_params=pltpu.CompilerParams(
@@ -639,10 +669,10 @@
     outs = pl.pallas_call(
         hand_out,
         out_shape=out_shapes(),
-        in_specs=[anywhere] * 5,
+        in_specs=[anywhere] * 3,
         out_specs=(anywhere,) * 5,
-        scratch_shapes=[pltpu.VMEM(a.shape, a.dtype) for a in out_shapes()]
-        + [pltpu.SemaphoreType.DMA((2, 5))],
+        scratch_shapes=[pltpu.VMEM(a.shape, a.dtype) for a in [*sums, *out_shapes()[1:]]]
+        + [pltpu.SemaphoreType.DMA((8,))],
         compiler_params=pltpu.CompilerParams(vmem_limit_bytes=60 * 1024 * 1024),
         name="hand_out",
     )(*outs)

time: 44.7 us -> 42.3 us (0.946)
  Pallas kernels: 43.9 us -> 41.5 us
    pallas_call x2, Pallas kernels: 43.9 us -> 41.5 us  [the longest x1 39.5 us: on_device(): pl.pallas_call(whole_kernel, out_shape=sums, in_specs=[anywhere] * 9, out...]
where the time goes in v4:
time: 42.3 us; the launch traced here: 42.1 us
  Pallas kernels  41.5 us (98%)
  between operations  0.64 us (2%)
    pallas_call x1, Pallas kernels, on_device(): pl.pallas_call(whole_kernel, out_shape=sums, in_specs=[anywhere] * 9, out...  39.5 us
    pallas_call x1, Pallas kernels, on_device(): pl.pallas_call(hand_out, out_shape=out_shapes(), in_specs=[anywhere] * 3,...  2.04 us

profile of v4, /device:TPU:1, one launch (start us, length us, event | category | flops | bytes accessed | tf_op | source)
XLA Modules:
  0.0 42.1 jit_solution(17308771379646616635)
XLA Ops:
  0.6 39.5 %whole.1 = (f32[3,16,16,128]{3,2,1,0:T(8,128)}, f32[64,128]{1,0:T(8,128)}, f32[2,512,128]{2,1,0:T(8,128)}) custom-call(f32[3,16,16,128]{3,2,1,0:T(8,128)} %refs_0_.1, bf16[8,8,64]{2,1,0:T(8,128)(2,1)} %refs_1_.1, bf16[64,81]{1,0:T(8,128)(2,1)} %refs_2_.1, bf16[64,1728]{1,0:T(8,128)(2,1)} %refs_3_.1, bf16[1,64]{1,0:T(2,128)(2,1)} %bitcast.6, ...), custom_call_target="tpu_custom_call" | custom-call | tf_op jit(solution)/shard_map/whole/pallas_call | solution.py:625
  40.1 2.0 %hand_out.1 = (f32[3,16,16,128]{3,2,1,0:T(8,128)}, f32[1,1,8]{2,1,0:T(1,128)}, f32[64,81]{1,0:T(8,128)}, f32[64,1728]{1,0:T(8,128)}, f32[1,64]{1,0:T(1,128)}) custom-call(f32[3,16,16,128]{3,2,1,0:T(8,128)} %get-tuple-element.13.u_source, f32[64,128]{1,0:T(8,128)} %get-tuple-element.14.f_source, f32[2,512,128]{2,1,0:T(8,128)} %get-tuple-element.15.source), custom_call_target="tpu_custom_call" | custom-call | tf_op jit(solution)/shard_map/hand_out/pallas_call | solution.py:669

commit v5 on v4

--- a/solution.py
+++ b/solution.py
@@ -101,8 +101,8 @@
             store[p, 1:9, :, j * 256 : (j + 1) * 256] = shift_y(whole, j - 1).astype(BF16)
 
 
-def rows_of(store, half, i):
-    return store[half, i : i + 8].reshape(512, 960)
+def rows_of(store, half, i, first=0, count=8):
+    return store[half, i + first : i + first + count].reshape(count * 64, 960)
 
 
 def place_weights(w_hidden, ahead, back):
@@ -139,16 +139,22 @@
             for z in range(4):
                 at = slice(z * 64, (z + 1) * 64)
                 for part in range(2):
-                    start = (j % 3) * 256 + part * 128
-                    ahead[half, j // 3, at, start : start + 128] = rows[z][part]
+                    if ahead is not None:
+                        start = (j % 3) * 256 + part * 128
+                        ahead[half, j // 3, at, start : start + 128] = rows[z][part]
+                        continue
                     start = (flip % 3) * 256 + z * 64
                     cut = slice(part * 128, (part + 1) * 128)
                     back[half, flip // 3, start : start + 64, cut] = rows[z][part]
+        if ahead is not None:
+            continue
         start = 768 + (flip % 3) * 64
         back[0, flip // 3, start : start + 64, 0:128] = zero
         back[0, flip // 3, start : start + 64, 128:256] = o_a
         back[1, flip // 3, start : start + 64, 0:128] = c_0
         back[1, flip // 3, start : start + 64, 128:256] = zero
+    if ahead is None:
+        return
     for half in range(2):
         for i in range(3):
             edge = jnp.where(low, lows[3 * i][half], highs[3 * i + 1][half]).astype(BF16)
@@ -224,7 +230,7 @@
 
     for n in (3, 0, 2, 8, 7, 1, 4, 5, 6):
         loads[n].wait()
-    place_weights(w_hidden, ahead, back)
+    place_weights(w_hidden, ahead, None)
     placed = dot(w_first[...], sel[...]).astype(BF16)
     for i in range(3):
         for zo in range(8):
@@ -275,27 +281,6 @@
     slope_one[...] = sig * (1.0 + pre * (1.0 - sig))
     acts = (pre * sig).astype(BF16).astype(F32)
     widen(wide_act, acts)
-    widen_pairs(pair_act, acts)
-
-    slot_of, base_of = (0, 0, 1, 2), (0, 16, 0, 0)
-    lane16 = lane_of((16, 128))
-
-    def pack_sides(c, field, wide):
-        for h in range(wide):
-            for i in range(16):
-                low, high = field[i, h : h + 1, :], field[i, 16 - wide + h : 17 - wide + h, :]
-                y_out[0, 2 * c + h, i : i + 1, :] = low
-                y_out[1, 2 * c + h, i : i + 1, :] = high
-        packed = None
-        for i in range(16):
-            g = base_of[c] + i
-            moved = pltpu.roll(field[i], 2 + 4 * g, 1)
-            packed = moved if packed is None else jnp.where(lane16 // 4 == g, moved, packed)
-        return packed
-
-    sides_of = [pack_sides(c, vel.at[c], 2) for c in range(3)]
-    z_out[0] = jnp.where(lane16 < 64, sides_of[0], sides_of[1])
-    z_out[1] = sides_of[2]
 
     wl = w_last[...].astype(F32)
     wl = jnp.concatenate([wl, wl, wl, wl], axis=1)
@@ -310,56 +295,44 @@
 
     loss = jnp.zeros((8, 128), F32)
     last = jnp.zeros((8, 256), F32)
-    deltas, parts = [], []
-    for half in range(2):
+
+    def second_layer(half, quarter):
         pre = None
         for i in range(3):
-            term = dot(rows_of(wide_act, half, i), ahead[half, i], NT)
+            term = dot(rows_of(wide_act, half, i, 4 * quarter, 4), ahead[half, i], NT)
             pre = term if pre is None else pre + term
+        return pre
+
+    turns = [(half, quarter) for half in range(2) for quarter in range(2)]
+    found = []
+    deltas, parts = [[], []], [[], [], [], []]
+    for turn, (half, quarter) in enumerate(turns):
+        while len(found) < min(4, turn + 1 + 2):
+            found.append(second_layer(*turns[len(found)]))
+            if len(found) == 2:
+                widen_pairs(pair_act, acts)
+        pre = found[turn]
+        here = slice(quarter * 256, quarter * 256 + 256)
         sig = 1.0 / (1.0 + jnp.exp(-pre))
         act = (pre * sig).astype(BF16)
         slope = sig * (1.0 + pre * (1.0 - sig))
         logits = dot(act, out_map, NT)
         small = jnp.exp(-jnp.abs(logits))
         eddy = 0.5 * (jnp.maximum(logits, 0.0) + jnp.log1p(small))
-        eddy_z[half] = eddy
+        eddy_z[half, here] = eddy
         gate = jnp.where(logits >= 0, 1.0, small) / (1.0 + small)
-        error = eddy - targets[:, half * 128 : half * 128 + 128]
-        loss = loss + jnp.sum((error * error).reshape(64, 8, 128), axis=0)
+        error = eddy - targets[here, half * 128 : half * 128 + 128]
+        loss = loss + jnp.sum((error * error).reshape(32, 8, 128), axis=0)
         d_logit = dot((error * gate * (1.0 / (256 * 512))).astype(BF16), repeat)
-        last = last + jnp.sum((d_logit * act.astype(F32)).reshape(64, 8, 256), axis=0)
+        last = last + jnp.sum((d_logit * act.astype(F32)).reshape(32, 8, 256), axis=0)
         delta = (wl * d_logit * slope).astype(BF16).astype(F32)
-        deltas.append(delta)
-        scaled = (delta.reshape(64, 8, 256) * times.reshape(1, 8, 1)).reshape(512, 256)
+        deltas[half].append(delta)
+        scaled = (delta.reshape(32, 8, 256) * times.reshape(1, 8, 1)).reshape(256, 256)
         high = scaled.astype(BF16)
         low = (scaled - high.astype(F32)).astype(BF16)
         for p in range(2):
             cut = slice(p * 128, p * 128 + 128)
-            parts.append(jnp.concatenate([high[:, cut].T, low[:, cut].T], axis=0))
-    widen(wide_del, jnp.concatenate(deltas, axis=1))
-
-    lane = lane_of((64, 128))
-    field = jnp.zeros((64, 128), F32)
-    for half in range(2):
-        for b in range(8):
-            part = eddy_z[half, pl.ds(b, 64, stride=8), :]
-            field = jnp.where(lane // 8 == 2 * b + half, part, field)
-    field = 0.02 + field
-    for i in range(8):
-        for dx in range(2):
-            for dy in range(2):
-                ext[3, 2 + 2 * i + dx, pl.ds(8 + dy, 8, stride=2), :] = field[i * 8 : i * 8 + 8]
-    z_out[2] = pack_sides(3, ext.at[3, 2:18, 8:24], 1)
-    pl.semaphore_wait(barrier, len(greeted))
-    rims = [
-        send(vel.at[:, 0:2], ext.at[0:3, 18:20, 8:24], x_down),
-        send(vel.at[:, 14:16], ext.at[0:3, 0:2, 8:24], x_up),
-        send(ext.at[3, 2:3, 8:24], ext.at[3, 18:19, 8:24], x_down),
-        send(ext.at[3, 17:18, 8:24], ext.at[3, 1:2, 8:24], x_up),
-        send(y_out.at[0], y_in.at[1], y_down),
-        send(y_out.at[1], y_in.at[0], y_up),
-        send(z_out, z_in, z_side),
-    ]
+            parts[2 * half + p].append(jnp.concatenate([high[:, cut].T, low[:, cut].T], axis=0))
 
     per_block = jnp.sum(loss, axis=1, keepdims=True) * (1.0 / (32 * 512))
     by_slot = jnp.sum(drawn * per_block, axis=0, keepdims=True)
@@ -375,14 +348,24 @@
     def column(t, value):
         sums[t // 7, (t % 7) * 64 : (t % 7) * 64 + 64, :] = value
 
+    lane = lane_of((64, 128))
     is_low = lane < 64
     held_a = None
-    for i in range(3):
+
+    def shift_sums(i):
         grad = None
         for p in range(4):
-            term = dot(parts[p], pair_act[p, i : i + 8].reshape(512, 768))
+            term = dot(
+                jnp.concatenate(parts[p], axis=1), pair_act[p, i : i + 8].reshape(512, 768)
+            )
             grad = term if grad is None else grad + term
-        grad = grad[:128] + grad[128:]
+        return grad[:128] + grad[128:]
+
+    grads = [shift_sums(0)]
+    for i in range(3):
+        if i < 2:
+            grads.append(shift_sums(i + 1))
+        grad = grads[i]
         for j in range(3):
             k = 3 * i + j
             g = [
@@ -401,10 +384,62 @@
                 column(t, jnp.where(is_low, held_a, ba))
                 column(t + 1, jnp.where(is_low, ba, pltpu.roll(c_low, 64, 1)))
     column(13, jnp.where(is_low, held_a, 0.0))
+    pl.semaphore_wait(barrier, len(greeted))
     first = send(sums.at[1 - core], half_in, other)
 
+    slot_of, base_of = (0, 0, 1, 2), (0, 16, 0, 0)
+    lane16 = lane_of((16, 128))
+
+    def pack_sides(c, field, wide):
+        for h in range(wide):
+            for i in range(16):
+                low, high = field[i, h : h + 1, :], field[i, 16 - wide + h : 17 - wide + h, :]
+                y_out[0, 2 * c + h, i : i + 1, :] = low
+                y_out[1, 2 * c + h, i : i + 1, :] = high
+        packed = None
+        for i in range(16):
+            g = base_of[c] + i
+            moved = pltpu.roll(field[i], 2 + 4 * g, 1)
+            packed = moved if packed is None else jnp.where(lane16 // 4 == g, moved, packed)
+        return packed
+
+    sides_of = [pack_sides(c, vel.at[c], 2) for c in range(3)]
+    z_out[0] = jnp.where(lane16 < 64, sides_of[0], sides_of[1])
+    z_out[1] = sides_of[2]
+
+    field = jnp.zeros((64, 128), F32)
+    for half in range(2):
+        for b in range(8):
+            part = eddy_z[half, pl.ds(b, 64, stride=8), :]
+            field = jnp.where(lane // 8 == 2 * b + half, part, field)
+    field = 0.02 + field
+    for i in range(8):
+        for dx in range(2):
+            for dy in range(2):
+                ext[3, 2 + 2 * i + dx, pl.ds(8 + dy, 8, stride=2), :] = field[i * 8 : i * 8 + 8]
+    z_out[2] = pack_sides(3, ext.at[3, 2:18, 8:24], 1)
+    rims = [
+        send(vel.at[:, 0:2], ext.at[0:3, 18:20, 8:24], x_down),
+        send(vel.at[:, 14:16], ext.at[0:3, 0:2, 8:24], x_up),
+        send(ext.at[3, 2:3, 8:24], ext.at[3, 18:19, 8:24], x_down),
+        send(ext.at[3, 17:18, 8:24], ext.at[3, 1:2, 8:24], x_up),
+        send(y_out.at[0], y_in.at[1], y_down),
+        send(y_out.at[1], y_in.at[0], y_up),
+        send(z_out, z_in, z_side),
+    ]
+
+    place_weights(w_hidden, None, back)
+    widen(wide_del, jnp.concatenate([jnp.concatenate(d, axis=0) for d in deltas], axis=1))
+    scatter = []
+    first.wait_recv()
+    half_sum[...] = sums[core] + half_in[...]
+    for s, (dy, dx) in enumerate(steps):
+        to, device = plane(dy, dx)
+        scatter.append(
+            send(half_sum.at[pl.ds(pl.multiple_of(to * 32, 32), 32)], chunk_in.at[s], device)
+        )
+
     firsts = []
-    scatter = []
     for half in range(2):
         d_act = None
         for i in range(3):
@@ -415,14 +450,6 @@
         high = scaled.astype(BF16)
         low = (scaled - high.astype(F32)).astype(BF16)
         firsts.append((high.T, low.T))
-        if half == 0:
-            first.wait_recv()
-            half_sum[...] = sums[core] + half_in[...]
-            for s, (dy, dx) in enumerate(steps):
-                to, device = plane(dy, dx)
-                scatter.append(
-                    send(half_sum.at[pl.ds(pl.multiple_of(to * 32, 32), 32)], chunk_in.at[s], device)
-                )
     lhs = jnp.concatenate([firsts[0][0], firsts[1][0], firsts[0][1], firsts[1][1]], axis=0)
     packed = jnp.zeros((64, 128), F32)
     for i in range(3):
@@ -535,7 +562,8 @@
     for d in range(1, 8):
         mine = mine + f_deep[d]
     f_total[own32, :] = mine
-    f_last = send(f_total.at[own32], f_total.at[own32], other)
+    f_last = send(f_total.at[own32], f_result.at[own32], other)
+    hand_over(f_total.at[own32], f_result.at[own32])
 
     across = []
     for dy in range(4):
@@ -546,7 +574,6 @@
         across.append(send(total.at[core, rows], result.at[core, rows], other))
     hand_over(total.at[core], result.at[core])
     f_last.wait_recv()
-    hand_over(f_total, f_result)
     for part in across:
         part.wait_recv()
     for part in started:
@@ -573,29 +600,28 @@
     u_held, f_held, held, slot_loss, grad_first, grad_hidden, grad_last, sems,
 ):
     gx, gy, role = lax.axis_index("gx"), lax.axis_index("gy"), lax.axis_index("role")
-    loads = [
-        pltpu.make_async_copy(source, held, sems.at[0]),
-        pltpu.make_async_copy(u_source, u_held, sems.at[1]),
-        pltpu.make_async_copy(f_source, f_held, sems.at[2]),
-    ]
-    stores = [
-        pltpu.make_async_copy(grad_hidden, hidden_result, sems.at[3]),
-        pltpu.make_async_copy(u_held, u_result, sems.at[4]),
-        pltpu.make_async_copy(grad_first, first_result, sems.at[5]),
-        pltpu.make_async_copy(grad_last, last_result, sems.at[6]),
-        pltpu.make_async_copy(slot_loss, loss_result, sems.at[7]),
+    loads = [pltpu.make_async_copy(source.at[n], held.at[n], sems.at[n]) for n in range(2)]
+    loads += [pltpu.make_async_copy(u_source.at[n], u_held.at[n], sems.at[2 + n]) for n in range(3)]
+    loads.append(pltpu.make_async_copy(f_source, f_held, sems.at[5]))
+    stores = [pltpu.make_async_copy(u_held.at[n], u_result.at[n], sems.at[6 + n]) for n in range(3)]
+    stores += [
+        pltpu.make_async_copy(grad_hidden, hidden_result, sems.at[9]),
+        pltpu.make_async_copy(grad_first, first_result, sems.at[10]),
+        pltpu.make_async_copy(grad_last, last_result, sems.at[11]),
+        pltpu.make_async_copy(slot_loss, loss_result, sems.at[12]),
     ]
     for load in loads:
         load.start()
-    loads[0].wait()
-    for t in range(14):
-        wide = 64 if t == 13 else 128
-        rows = slice((t % 7) * 64, (t % 7) * 64 + 64)
-        grad_hidden[:, t * 128 : t * 128 + wide] = held[t // 7, rows, :wide]
-    stores[0].start()
-    loads[1].wait()
-    stores[1].start()
-    loads[2].wait()
+    for half in range(2):
+        loads[half].wait()
+        for t in range(7):
+            start, width = half * 896 + t * 128, 64 if half == 1 and t == 6 else 128
+            grad_hidden[:, start : start + width] = held[half, t * 64 : t * 64 + 64, :width]
+    stores[3].start()
+    for n in range(3):
+        loads[2 + n].wait()
+        stores[n].start()
+    loads[5].wait()
     grad_first[...] = f_held[:, :81]
     grad_last[...] = held[1, 448:449, :64]
     losses = held[0, 448:464, :]
@@ -604,7 +630,7 @@
     losses = jnp.sum(losses, axis=0, keepdims=True)
     losses = pltpu.roll(losses, (128 - (gx % 16) * 8) % 128, 1)
     slot_loss[0] = losses[:, :8]
-    for store in stores[2:]:
+    for store in stores[4:]:
         store.start()
     for store in stores:
         store.wait()
@@ -672,7 +698,7 @@
         in_specs=[anywhere] * 3,
         out_specs=(anywhere,) * 5,
         scratch_shapes=[pltpu.VMEM(a.shape, a.dtype) for a in [*sums, *out_shapes()[1:]]]
-        + [pltpu.SemaphoreType.DMA((8,))],
+        + [pltpu.SemaphoreType.DMA((13,))],
         compiler_params=pltpu.CompilerParams(vmem_limit_bytes=60 * 1024 * 1024),
         name="hand_out",
     )(*outs)

time: 42.3 us -> 39.9 us (0.943)
  Pallas kernels: 41.5 us -> 39.2 us
    pallas_call x1, Pallas kernels: 39.5 us -> 37.1 us  [on_device(): pl.pallas_call(whole_kernel, out_shape=sums, in_specs=[anywhere] * 9, out...]
where the time goes in v5:
time: 39.9 us; the launch traced here: 39.8 us
  Pallas kernels  39.2 us (98%)
  between operations  0.64 us (2%)
    pallas_call x1, Pallas kernels, on_device(): pl.pallas_call(whole_kernel, out_shape=sums, in_specs=[anywhere] * 9, out...  37.1 us
    pallas_call x1, Pallas kernels, on_device(): pl.pallas_call(hand_out, out_shape=out_shapes(), in_specs=[anywhere] * 3,...  2.06 us

profile of v5, /device:TPU:1, one launch (start us, length us, event | category | flops | bytes accessed | tf_op | source)
XLA Modules:
  0.0 39.8 jit_solution(8617847728646487959)
XLA Ops:
  0.6 37.1 %whole.1 = (f32[3,16,16,128]{3,2,1,0:T(8,128)}, f32[64,128]{1,0:T(8,128)}, f32[2,512,128]{2,1,0:T(8,128)}) custom-call(f32[3,16,16,128]{3,2,1,0:T(8,128)} %refs_0_.1, bf16[8,8,64]{2,1,0:T(8,128)(2,1)} %refs_1_.1, bf16[64,81]{1,0:T(8,128)(2,1)} %refs_2_.1, bf16[64,1728]{1,0:T(8,128)(2,1)} %refs_3_.1, bf16[1,64]{1,0:T(2,128)(2,1)} %bitcast.6, ...), custom_call_target="tpu_custom_call" | custom-call | tf_op jit(solution)/shard_map/whole/pallas_call | solution.py:651
  37.7 2.1 %hand_out.1 = (f32[3,16,16,128]{3,2,1,0:T(8,128)}, f32[1,1,8]{2,1,0:T(1,128)}, f32[64,81]{1,0:T(8,128)}, f32[64,1728]{1,0:T(8,128)}, f32[1,64]{1,0:T(1,128)}) custom-call(f32[3,16,16,128]{3,2,1,0:T(8,128)} %get-tuple-element.13.u_source, f32[64,128]{1,0:T(8,128)} %get-tuple-element.14.f_source, f32[2,512,128]{2,1,0:T(8,128)} %get-tuple-element.15.source), custom_call_target="tpu_custom_call" | custom-call | tf_op jit(solution)/shard_map/hand_out/pallas_call | solution.py:695

commit v6 on v5

--- a/solution.py
+++ b/solution.py
@@ -228,9 +228,10 @@
         part.start()
         return part
 
-    for n in (3, 0, 2, 8, 7, 1, 4, 5, 6):
+    loads[3].wait()
+    place_weights(w_hidden, ahead, None)
+    for n in (0, 2, 8, 7, 1, 4, 5, 6):
         loads[n].wait()
-    place_weights(w_hidden, ahead, None)
     placed = dot(w_first[...], sel[...]).astype(BF16)
     for i in range(3):
         for zo in range(8):
@@ -439,12 +440,14 @@
             send(half_sum.at[pl.ds(pl.multiple_of(to * 32, 32), 32)], chunk_in.at[s], device)
         )
 
-    firsts = []
+    firsts, d_acts = [], []
     for half in range(2):
         d_act = None
         for i in range(3):
             term = dot(rows_of(wide_del, half, i), back[half, i])
             d_act = term if d_act is None else d_act + term
+        d_acts.append(d_act)
+    for half, d_act in enumerate(d_acts):
         d_first = (d_act * slope_one[:, half * 256 : half * 256 + 256]).astype(BF16).astype(F32)
         scaled = (d_first.reshape(64, 8, 256) * times.reshape(1, 8, 1)).reshape(512, 256)
         high = scaled.astype(BF16)
@@ -487,6 +490,26 @@
     chunk_sum[...] = mine
     deep_in[depth] = mine
     deep = [send(chunk_sum, deep_in.at[depth], device) for device in deeper]
+
+    for part in deep:
+        part.wait_recv()
+    mine = deep_in[0]
+    for d in range(1, 8):
+        mine = mine + deep_in[d]
+    own = pl.ds(pl.multiple_of(spot * 32, 32), 32)
+    total[core, own, :] = mine
+    gather = [
+        send(total.at[core, own], total.at[core, own], plane(dy, dx)[1]) for dy, dx in steps
+    ]
+
+    for part in f_across:
+        part.wait_recv()
+    mine = f_plane[0]
+    for s in range(1, 16):
+        mine = mine + f_plane[s]
+    f_mid[...] = mine
+    f_deep[depth] = mine
+    f_planes = [send(f_mid, f_deep.at[depth], device) for device in deeper]
 
     for rim in rims:
         rim.wait_recv()
@@ -535,26 +558,6 @@
 
     lax.fori_loop(0, 16, row, 0)
     hand_over(u_next, u_result)
-
-    for part in f_across:
-        part.wait_recv()
-    mine = f_plane[0]
-    for s in range(1, 16):
-        mine = mine + f_plane[s]
-    f_mid[...] = mine
-    f_deep[depth] = mine
-    f_planes = [send(f_mid, f_deep.at[depth], device) for device in deeper]
-
-    for part in deep:
-        part.wait_recv()
-    mine = deep_in[0]
-    for d in range(1, 8):
-        mine = mine + deep_in[d]
-    own = pl.ds(pl.multiple_of(spot * 32, 32), 32)
-    total[core, own, :] = mine
-    gather = [
-        send(total.at[core, own], total.at[core, own], plane(dy, dx)[1]) for dy, dx in steps
-    ]
 
     for part in f_planes:
         part.wait_recv()

time: 39.9 us -> 39.6 us (level)
  Pallas kernels: 39.2 us -> 38.8 us
where the time goes in v6:
time: 39.6 us; the launch traced here: 39.5 us
  Pallas kernels  38.8 us (98%)
  between operations  0.64 us (2%)
    pallas_call x1, Pallas kernels, on_device(): pl.pallas_call(whole_kernel, out_shape=sums, in_specs=[anywhere] * 9, out...  36.8 us
    pallas_call x1, Pallas kernels, on_device(): pl.pallas_call(hand_out, out_shape=out_shapes(), in_specs=[anywhere] * 3,...  2.06 us

profile of v6, /device:TPU:1, one launch (start us, length us, event | category | flops | bytes accessed | tf_op | source)
XLA Modules:
  0.0 39.5 jit_solution(13359712365617564106)
XLA Ops:
  0.6 36.8 %whole.1 = (f32[3,16,16,128]{3,2,1,0:T(8,128)}, f32[64,128]{1,0:T(8,128)}, f32[2,512,128]{2,1,0:T(8,128)}) custom-call(f32[3,16,16,128]{3,2,1,0:T(8,128)} %refs_0_.1, bf16[8,8,64]{2,1,0:T(8,128)(2,1)} %refs_1_.1, bf16[64,81]{1,0:T(8,128)(2,1)} %refs_2_.1, bf16[64,1728]{1,0:T(8,128)(2,1)} %refs_3_.1, bf16[1,64]{1,0:T(2,128)(2,1)} %bitcast.6, ...), custom_call_target="tpu_custom_call" | custom-call | tf_op jit(solution)/shard_map/whole/pallas_call | solution.py:654
  37.4 2.1 %hand_out.1 = (f32[3,16,16,128]{3,2,1,0:T(8,128)}, f32[1,1,8]{2,1,0:T(1,128)}, f32[64,81]{1,0:T(8,128)}, f32[64,1728]{1,0:T(8,128)}, f32[1,64]{1,0:T(1,128)}) custom-call(f32[3,16,16,128]{3,2,1,0:T(8,128)} %get-tuple-element.13.u_source, f32[64,128]{1,0:T(8,128)} %get-tuple-element.14.f_source, f32[2,512,128]{2,1,0:T(8,128)} %get-tuple-element.15.source), custom_call_target="tpu_custom_call" | custom-call | tf_op jit(solution)/shard_map/hand_out/pallas_call | solution.py:698
